TPU v7x, 32 devices: a whole 2x2x4 slice. The times are simulated.
32 devices in a mesh: dp: 16 (over z, x, core), tensor: 2 (over y).
Axes of the slice: x: 2, y: 2, z: 4, core: 2. Of those that a mesh axis runs over, the one named last changes fastest.
Arguments:
- frames: bfloat16 [32, 1024, 512], P('dp', 'tensor'), may hold values from -6 to 6
- codes: int32 [32, 1024], P('dp', 'tensor'), may hold values from 0 to 8191
- clip_frames: int32 [8], replicated, may hold values from 1 to 12, 32 in all
- out_cotangent: bfloat16 [32, 1024, 512], P('dp', 'tensor'), may hold values from -6 to 6
- heads_weight: float32 [2, 3, 512, 512], P(None, None, 'dp', 'tensor'), may hold values from -0.25 to 0.25
- merge_weight: float32 [2, 512, 512], P(None, 'tensor', 'dp'), may hold values from -6 to 6
- expand_weight: float32 [2, 512, 2048], P(None, 'dp', 'tensor'), may hold values from -0.25 to 0.25
- shrink_weight: float32 [2, 2048, 512], P(None, 'tensor', 'dp'), may hold values from -0.125 to 0.125
- vectors: float32 [15, 512], P(None, ('dp', 'tensor')), may hold values from -0.9 to 2.7, as said below
- encode_weight: float32 [512, 32], P(('dp', 'tensor')), may hold values from -0.25 to 0.25
- codebook: float32 [8192, 32], P(('dp', 'tensor')), may hold values from -6 to 6
- decode_weight: float32 [32, 512], P(None, ('dp', 'tensor')), may hold values from -1 to 1
- heads_first: float32 [2, 3, 512, 512], P(None, None, 'dp', 'tensor'), may hold values from -0.00024414062 to 0.00024414062
- merge_first: float32 [2, 512, 512], P(None, 'tensor', 'dp'), may hold values from -5.340576e-05 to 5.340576e-05
- expand_first: float32 [2, 512, 2048], P(None, 'dp', 'tensor'), may hold values from -3.8146973e-05 to 3.8146973e-05
- shrink_first: float32 [2, 2048, 512], P(None, 'tensor', 'dp'), may hold values from -5.340576e-05 to 5.340576e-05
- vectors_first: float32 [15, 512], P(None, ('dp', 'tensor')), may hold values from -0.00024414062 to 0.00024414062
- encode_first: float32 [512, 32], P(('dp', 'tensor')), may hold values from -0.00024414062 to 0.00024414062
- codebook_first: float32 [8192, 32], P(('dp', 'tensor')), may hold values from -6.67572e-06 to 6.67572e-06
- decode_first: float32 [32, 512], P(None, ('dp', 'tensor')), may hold values from -0.00024414062 to 0.00024414062
- heads_second: float32 [2, 3, 512, 512], P(None, None, 'dp', 'tensor'), may hold values from 3.94295e-09 to 6.3693804e-08
- merge_second: float32 [2, 512, 512], P(None, 'tensor', 'dp'), may hold values from 1.7743274e-10 to 2.8662213e-09
- expand_second: float32 [2, 512, 2048], P(None, 'dp', 'tensor'), may hold values from 9.8573746e-11 to 1.5923451e-09
- shrink_second: float32 [2, 2048, 512], P(None, 'tensor', 'dp'), may hold values from 1.5771799e-10 to 2.5477522e-09
- vectors_second: float32 [15, 512], P(None, ('dp', 'tensor')), may hold values from 3.94295e-09 to 6.3693804e-08
- encode_second: float32 [512, 32], P(('dp', 'tensor')), may hold values from 3.94295e-09 to 6.3693804e-08
- codebook_second: float32 [8192, 32], P(('dp', 'tensor')), may hold values from 2.36577e-12 to 3.821628e-11
- decode_second: float32 [32, 512], P(None, ('dp', 'tensor')), may hold values from 3.94295e-09 to 6.3693804e-08
Outputs:
- decoded: float32 [32, 1024, 512], P('dp', 'tensor')
- frames_grad: float32 [32, 1024, 512], P('dp', 'tensor')
- norm_before: float32 [], replicated
- heads_mean: float32 [2, 3, 512, 512], P(None, None, 'dp', 'tensor')
- heads_square: float32 [2, 3, 512, 512], P(None, None, 'dp', 'tensor')
- heads_master: float32 [2, 3, 512, 512], P(None, None, 'dp', 'tensor')
- heads_copy: bfloat16 [2, 3, 512, 512], P(None, None, 'dp', 'tensor')
- merge_mean: float32 [2, 512, 512], P(None, 'tensor', 'dp')
- merge_square: float32 [2, 512, 512], P(None, 'tensor', 'dp')
- merge_master: float32 [2, 512, 512], P(None, 'tensor', 'dp')
- merge_copy: bfloat16 [2, 512, 512], P(None, 'tensor', 'dp')
- expand_mean: float32 [2, 512, 2048], P(None, 'dp', 'tensor')
- expand_square: float32 [2, 512, 2048], P(None, 'dp', 'tensor')
- expand_master: float32 [2, 512, 2048], P(None, 'dp', 'tensor')
- expand_copy: bfloat16 [2, 512, 2048], P(None, 'dp', 'tensor')
- shrink_mean: float32 [2, 2048, 512], P(None, 'tensor', 'dp')
- shrink_square: float32 [2, 2048, 512], P(None, 'tensor', 'dp')
- shrink_master: float32 [2, 2048, 512], P(None, 'tensor', 'dp')
- shrink_copy: bfloat16 [2, 2048, 512], P(None, 'tensor', 'dp')
- vectors_mean: float32 [15, 512], P(None, ('dp', 'tensor'))
- vectors_square: float32 [15, 512], P(None, ('dp', 'tensor'))
- vectors_master: float32 [15, 512], P(None, ('dp', 'tensor'))
- vectors_copy: bfloat16 [15, 512], P(None, ('dp', 'tensor'))
- encode_mean: float32 [512, 32], P(('dp', 'tensor'))
- encode_square: float32 [512, 32], P(('dp', 'tensor'))
- encode_master: float32 [512, 32], P(('dp', 'tensor'))
- encode_copy: bfloat16 [512, 32], P(('dp', 'tensor'))
- codebook_mean: float32 [8192, 32], P(('dp', 'tensor'))
- codebook_square: float32 [8192, 32], P(('dp', 'tensor'))
- codebook_master: float32 [8192, 32], P(('dp', 'tensor'))
- codebook_copy: bfloat16 [8192, 32], P(('dp', 'tensor'))
- decode_mean: float32 [32, 512], P(None, ('dp', 'tensor'))
- decode_square: float32 [32, 512], P(None, ('dp', 'tensor'))
- decode_master: float32 [32, 512], P(None, ('dp', 'tensor'))
- decode_copy: bfloat16 [32, 512], P(None, ('dp', 'tensor'))
Inputs may be any that keep to these rules, and one draw needn't show every extreme that they name: Clip c holds clip_frames[c] consecutive frames, clips in order over all 32 frames; the counts sum to 32 and the largest is exactly 12. `vectors`: rows 0, 3, 6, 9 and 12 are positive gains.
All inputs are finite; a program needn't handle non-finite values.
Results may differ from a plain program's by a relative error of at most 0.015.
The roundings to bfloat16 on the way count: a program that leaves them out, or rounds other values in their place, can miss the bound.
Values may be sent and summed in bfloat16 or wider, within the bound.
A program may use at most 256 MiB of HBM per device.

v0:
```python
import jax
import jax.numpy as jnp
from jax import lax
from jax.sharding import PartitionSpec as P

HEAD_DIM = 64
STEP = 10


EPS_NORM = 1e-05
EPS_UNIT = 1e-06
COMMIT_WEIGHT = 100.0
MAX_NORM = 1.0
MEAN_DECAY = 0.9
SQUARE_DECAY = 0.95
ADAM_EPS = 1e-08
RATES = (0.1, 0.5, 0.1, 0.05, 1.0, 0.1, 1.0, 0.3)
DECAYS = (0.1, 0.1, 0.1, 0.1, 0.0, 0.1, 0.1, 0.1)


def layer_norm(token_rows, gain_row, shift_row):
    center = token_rows - jnp.mean(token_rows, axis=-1, keepdims=True)
    spread = jnp.mean(center * center, axis=-1, keepdims=True)
    return center * lax.rsqrt(spread + EPS_NORM) * gain_row + shift_row


def unit_rows(vectors_in):
    return vectors_in * lax.rsqrt(
        jnp.sum(vectors_in * vectors_in, axis=-1, keepdims=True) + EPS_UNIT
    )


def gelu_tanh(values):
    return jax.nn.gelu(values, approximate=True)


def fast_dot(formula, first_arg, second_arg):
    return jnp.einsum(formula, first_arg, second_arg, preferred_element_type=jnp.float32)


def exact_dot(formula, first_arg, second_arg):
    return jnp.einsum(
        formula,
        first_arg,
        second_arg,
        precision=lax.Precision.HIGHEST,
        preferred_element_type=jnp.float32,
    )


def gather_tensor(local_rows):
    return lax.all_gather(local_rows, "tensor", axis=0, tiled=True)


def gather_cotangent(local_rows):
    return lax.all_gather(local_rows.astype(jnp.bfloat16), "tensor", axis=0, tiled=True)


def attend_forward(projected, block_rows):
    length = projected.shape[1]
    head_count = projected.shape[2] // HEAD_DIM
    queries = projected[0].reshape(length, head_count, HEAD_DIM)
    keys_all = projected[1].reshape(length, head_count, HEAD_DIM)
    values_all = projected[2].reshape(length, head_count, HEAD_DIM)
    outputs = []
    log_parts = []
    for first_row in range(0, length, block_rows):
        query_block = queries[first_row : first_row + block_rows]
        scores = fast_dot("qhd,khd->hqk", query_block, keys_all) * HEAD_DIM ** (-0.5)
        top_score = jnp.max(scores, axis=-1, keepdims=True)
        exponent = jnp.exp(scores - top_score)
        totals = jnp.sum(exponent, axis=-1, keepdims=True)
        attend = (exponent / totals).astype(jnp.bfloat16)
        block_out = fast_dot("hqk,khd->qhd", attend, values_all).astype(jnp.bfloat16)
        outputs.append(block_out.reshape(block_rows, head_count * HEAD_DIM))
        log_parts.append((top_score + jnp.log(totals))[..., 0])
    return (jnp.concatenate(outputs, 0), jnp.concatenate(log_parts, 1))


def attend_backward(projected, log_sums, dmixture, block_rows):
    length = projected.shape[1]
    head_count = projected.shape[2] // HEAD_DIM
    queries = projected[0].reshape(length, head_count, HEAD_DIM)
    keys_all = projected[1].reshape(length, head_count, HEAD_DIM)
    values_all = projected[2].reshape(length, head_count, HEAD_DIM)
    dmix_heads = dmixture.reshape(length, head_count, HEAD_DIM)
    scale = HEAD_DIM ** (-0.5)
    dkeys_all = jnp.zeros((length, head_count, HEAD_DIM), jnp.float32)
    dvalues = jnp.zeros((length, head_count, HEAD_DIM), jnp.float32)
    dqueries = []
    for first_row in range(0, length, block_rows):
        query_block = queries[first_row : first_row + block_rows]
        dmix_block = dmix_heads[first_row : first_row + block_rows]
        scores = fast_dot("qhd,khd->hqk", query_block, keys_all) * scale
        attend = jnp.exp(scores - log_sums[:, first_row : first_row + block_rows, None])
        dvalues = dvalues + fast_dot("hqk,qhd->khd", attend.astype(jnp.bfloat16), dmix_block)
        dattend = fast_dot("qhd,khd->hqk", dmix_block, values_all)
        inner_sum = jnp.sum(attend * dattend, axis=-1, keepdims=True)
        dscores = (attend * (dattend - inner_sum)).astype(jnp.bfloat16)
        dqueries.append(fast_dot("hqk,khd->qhd", dscores, keys_all) * scale)
        dkeys_all = dkeys_all + fast_dot("hqk,qhd->khd", dscores, query_block) * scale
    width = head_count * HEAD_DIM
    stacked = jnp.stack(
        [
            jnp.concatenate(dqueries, 0).reshape(length, width),
            dkeys_all.reshape(length, width),
            dvalues.reshape(length, width),
        ]
    )
    return stacked.astype(jnp.bfloat16)


def block_forward(token_rows, weight_set, vector_rows, block_rows):
    head_proj, merge_proj, expand_proj, shrink_proj = weight_set
    rows_here = token_rows.shape[0]
    normed = layer_norm(token_rows, vector_rows[0], vector_rows[1]).astype(jnp.bfloat16)
    normed_all = gather_tensor(normed)
    projected = fast_dot("td,cde->cte", normed_all, head_proj).astype(jnp.bfloat16)
    mixture, log_sums = attend_forward(projected, block_rows)
    merged = lax.psum_scatter(
        fast_dot(
            "te,ed->td",
            lax.slice_in_dim(mixture, 0, rows_here * lax.axis_size("tensor"), axis=0),
            merge_proj,
        ).astype(jnp.bfloat16),
        "tensor",
        scatter_dimension=0,
        tiled=True,
    ).astype(jnp.float32)
    hidden = token_rows + merged + vector_rows[2]
    normed_mlp = layer_norm(hidden, vector_rows[3], vector_rows[4]).astype(jnp.bfloat16)
    normed_mlp_all = gather_tensor(normed_mlp)
    expanded = fast_dot("td,df->tf", normed_mlp_all, expand_proj)
    active = gelu_tanh(expanded).astype(jnp.bfloat16)
    shrunk = lax.psum_scatter(
        fast_dot(
            "tf,fd->td",
            lax.slice_in_dim(active, 0, rows_here * lax.axis_size("tensor"), axis=0),
            shrink_proj,
        ).astype(jnp.bfloat16),
        "tensor",
        scatter_dimension=0,
        tiled=True,
    ).astype(jnp.float32)
    output = hidden + shrunk + vector_rows[5]
    kept_values = (
        token_rows,
        hidden,
        normed,
        normed_mlp,
        normed_all,
        normed_mlp_all,
        projected,
        mixture,
        log_sums,
        expanded,
        active,
    )
    return (output, kept_values)


def block_backward(kept_values, grad_out, weight_set, vector_rows, block_rows):
    head_proj, merge_proj, expand_proj, shrink_proj = weight_set
    (
        token_rows,
        hidden,
        normed,
        normed_mlp,
        normed_all,
        normed_mlp_all,
        projected,
        mixture,
        log_sums,
        expanded,
        active,
    ) = kept_values
    rows_here = grad_out.shape[0]
    dshrink_all = gather_cotangent(grad_out)
    dshrink = fast_dot("tf,td->fd", active, dshrink_all)
    dactive = fast_dot("td,fd->tf", dshrink_all, shrink_proj)
    dexpanded = jax.vjp(gelu_tanh, expanded)[1](dactive)[0].astype(jnp.bfloat16)
    dexpand = fast_dot("td,tf->df", normed_mlp_all, dexpanded)
    dnormed_mlp = lax.psum_scatter(
        fast_dot(
            "tf,df->td",
            lax.slice_in_dim(dexpanded, 0, rows_here * lax.axis_size("tensor"), axis=0),
            expand_proj,
        ).astype(jnp.bfloat16),
        "tensor",
        scatter_dimension=0,
        tiled=True,
    ).astype(jnp.float32)
    pullback_mlp = jax.vjp(layer_norm, hidden, vector_rows[3], vector_rows[4])[1]
    dhidden_norm, gain_grad_mlp, shift_grad_mlp = pullback_mlp(dnormed_mlp)
    dhidden = grad_out + dhidden_norm
    dmerge_all = gather_cotangent(dhidden)
    dmerge = fast_dot("te,td->ed", mixture, dmerge_all)
    dmixture = fast_dot("td,ed->te", dmerge_all, merge_proj).astype(jnp.bfloat16)
    dprojected = attend_backward(projected, log_sums, dmixture, block_rows)
    dheads = fast_dot("td,cte->cde", normed_all, dprojected)
    dnormed = lax.psum_scatter(
        fast_dot(
            "cte,cde->td",
            lax.slice_in_dim(dprojected, 0, rows_here * lax.axis_size("tensor"), axis=1),
            head_proj,
        ).astype(jnp.bfloat16),
        "tensor",
        scatter_dimension=0,
        tiled=True,
    ).astype(jnp.float32)
    pullback_attn = jax.vjp(layer_norm, token_rows, vector_rows[0], vector_rows[1])[1]
    dtoken_norm, gain_grad, shift_grad = pullback_attn(dnormed)
    dvectors = jnp.stack(
        [
            gain_grad,
            shift_grad,
            jnp.sum(dhidden, axis=0),
            gain_grad_mlp,
            shift_grad_mlp,
            jnp.sum(grad_out, axis=0),
        ]
    )
    return (dhidden + dtoken_norm, (dheads, dmerge, dexpand, dshrink), dvectors)


def quantize_forward(encoded, code_ids, small_set):
    vector_set, encode_low, codebook_low, decode_low = small_set
    normed = layer_norm(encoded, vector_set[12], vector_set[13]).astype(jnp.bfloat16)
    latent_raw = fast_dot("td,dc->tc", normed, encode_low)
    latent = unit_rows(latent_raw)
    entries = jnp.take(codebook_low, code_ids, axis=0).astype(jnp.float32)
    chosen = unit_rows(entries)
    chosen_low = chosen.astype(jnp.bfloat16)
    started = fast_dot("tc,cd->td", chosen_low, decode_low) + vector_set[14]
    return (started, (encoded, normed, latent_raw, latent, entries, chosen, chosen_low))


def quantize_backward(kept_values, dstarted, code_ids, clip_weight, small_set):
    vector_set, encode_low, codebook_low, decode_low = small_set
    encoded, normed, latent_raw, latent, entries, chosen, chosen_low = kept_values
    dstart_bias = jnp.sum(dstarted, axis=0)
    ddecode = exact_dot("tc,td->cd", chosen_low.astype(jnp.float32), dstarted)
    pulled = 2.0 * COMMIT_WEIGHT * clip_weight * (latent - chosen)
    dchosen = exact_dot("td,cd->tc", dstarted, decode_low.astype(jnp.float32)) - pulled
    dentries = jax.vjp(unit_rows, entries)[1](dchosen)[0]
    dcodebook = jax.ops.segment_sum(dentries, code_ids, num_segments=codebook_low.shape[0])
    dlatent_raw = jax.vjp(unit_rows, latent_raw)[1](pulled)[0]
    dencode = exact_dot("td,tc->dc", normed.astype(jnp.float32), dlatent_raw)
    dnormed = exact_dot("tc,dc->td", dlatent_raw, encode_low.astype(jnp.float32))
    pullback = jax.vjp(layer_norm, encoded, vector_set[12], vector_set[13])[1]
    dencoded, gain_grad, shift_grad = pullback(dnormed)
    return (
        dencoded,
        (jnp.stack([gain_grad, shift_grad, dstart_bias]), dencode, dcodebook, ddecode),
    )


def adam_update(master, gradient, first_state, second_state, step_rate, decay_rate):
    mean_new = MEAN_DECAY * first_state + (1.0 - MEAN_DECAY) * gradient
    square_new = SQUARE_DECAY * second_state + (1.0 - SQUARE_DECAY) * gradient * gradient
    normal_step = (
        mean_new
        / (1.0 - MEAN_DECAY**STEP)
        / (jnp.sqrt(square_new / (1.0 - SQUARE_DECAY**STEP)) + ADAM_EPS)
    )
    updated = master - step_rate * (normal_step + decay_rate * master)
    return (mean_new, square_new, updated, updated.astype(jnp.bfloat16))


def local(
    frames,
    codes,
    clip_frames,
    out_cotangent,
    heads_weight,
    merge_weight,
    expand_weight,
    shrink_weight,
    vectors,
    encode_weight,
    codebook,
    decode_weight,
    heads_first,
    merge_first,
    expand_first,
    shrink_first,
    vectors_first,
    encode_first,
    codebook_first,
    decode_first,
    heads_second,
    merge_second,
    expand_second,
    shrink_second,
    vectors_second,
    encode_second,
    codebook_second,
    decode_second,
):
    block_low = (
        lax.all_gather(heads_weight.astype(jnp.bfloat16), "dp", axis=2, tiled=True),
        lax.all_gather(merge_weight.astype(jnp.bfloat16), "dp", axis=2, tiled=True),
        lax.all_gather(expand_weight.astype(jnp.bfloat16), "dp", axis=1, tiled=True),
        lax.all_gather(shrink_weight.astype(jnp.bfloat16), "dp", axis=2, tiled=True),
    )
    small_low = (
        lax.all_gather(vectors.astype(jnp.bfloat16), ("dp", "tensor"), axis=1, tiled=True),
        lax.all_gather(encode_weight.astype(jnp.bfloat16), ("dp", "tensor"), axis=0, tiled=True),
        lax.all_gather(codebook.astype(jnp.bfloat16), ("dp", "tensor"), axis=0, tiled=True),
        lax.all_gather(decode_weight.astype(jnp.bfloat16), ("dp", "tensor"), axis=1, tiled=True),
    )
    vector_set = small_low[0].astype(jnp.float32)
    small_set = (vector_set, small_low[1], small_low[2], small_low[3])
    micro_count = frames.shape[0]
    frame_len = frames.shape[1] * lax.axis_size("tensor")
    block_rows = min(512, frame_len)
    clip_ends = jnp.cumsum(clip_frames)
    frame_ids = lax.axis_index("dp") * micro_count + jnp.arange(micro_count, dtype=jnp.int32)
    clip_ids = jnp.sum((clip_ends[None, :] <= frame_ids[:, None]).astype(jnp.int32), axis=1)
    clip_slots = jnp.arange(clip_frames.shape[0], dtype=jnp.int32)
    clip_counts = jnp.sum(
        jnp.where(clip_slots[None, :] == clip_ids[:, None], clip_frames[None, :], 0), axis=1
    )
    clip_weights = 1.0 / clip_counts.astype(jnp.float32)
    encoder_set = tuple((gathered[0] for gathered in block_low))
    decoder_set = tuple((gathered[1] for gathered in block_low))
    block_init = tuple((jnp.zeros(gathered.shape, jnp.float32) for gathered in block_low))
    small_init = tuple((jnp.zeros(gathered.shape, jnp.float32) for gathered in small_low))

    def one_micro(carried, inputs):
        block_acc, small_acc = carried
        frame_rows, code_ids, cotangent, clip_weight = inputs
        encoded, kept_encoder = block_forward(
            frame_rows.astype(jnp.float32), encoder_set, vector_set[0:6], block_rows
        )
        started, kept_quant = quantize_forward(encoded, code_ids, small_set)
        decoded, kept_decoder = block_forward(started, decoder_set, vector_set[6:12], block_rows)
        dstarted, decoder_grads, decoder_vectors = block_backward(
            kept_decoder, cotangent.astype(jnp.float32), decoder_set, vector_set[6:12], block_rows
        )
        dencoded, quant_grads = quantize_backward(
            kept_quant, dstarted, code_ids, clip_weight, small_set
        )
        dframe, encoder_grads, encoder_vectors = block_backward(
            kept_encoder, dencoded, encoder_set, vector_set[0:6], block_rows
        )
        block_new = tuple(
            (
                jnp.stack([first_part, second_part])
                for first_part, second_part in zip(encoder_grads, decoder_grads)
            )
        )
        small_new = (
            jnp.concatenate([encoder_vectors, decoder_vectors, quant_grads[0]], axis=0),
            quant_grads[1],
            quant_grads[2],
            quant_grads[3],
        )
        block_acc = tuple((running + addition for running, addition in zip(block_acc, block_new)))
        small_acc = tuple((running + addition for running, addition in zip(small_acc, small_new)))
        return ((block_acc, small_acc), (decoded, dframe))

    (block_acc, small_acc), (decoded_all, frame_grads) = lax.scan(
        one_micro, (block_init, small_init), (frames, codes, out_cotangent, clip_weights)
    )
    block_grads = (
        lax.psum_scatter(block_acc[0], "dp", scatter_dimension=2, tiled=True),
        lax.psum_scatter(block_acc[1], "dp", scatter_dimension=2, tiled=True),
        lax.psum_scatter(block_acc[2], "dp", scatter_dimension=1, tiled=True),
        lax.psum_scatter(block_acc[3], "dp", scatter_dimension=2, tiled=True),
    )
    small_grads = (
        lax.psum_scatter(small_acc[0], ("dp", "tensor"), scatter_dimension=1, tiled=True),
        lax.psum_scatter(small_acc[1], ("dp", "tensor"), scatter_dimension=0, tiled=True),
        lax.psum_scatter(small_acc[2], ("dp", "tensor"), scatter_dimension=0, tiled=True),
        lax.psum_scatter(small_acc[3], ("dp", "tensor"), scatter_dimension=1, tiled=True),
    )
    gradients = tuple(block_grads) + tuple(small_grads)
    local_squares = jnp.zeros((), jnp.float32)
    for gradient in gradients:
        local_squares = local_squares + jnp.sum(gradient * gradient)
    norm_before = jnp.sqrt(lax.psum(local_squares, ("dp", "tensor")))
    factor = MAX_NORM / jnp.maximum(norm_before, MAX_NORM)
    masters = (
        heads_weight,
        merge_weight,
        expand_weight,
        shrink_weight,
        vectors,
        encode_weight,
        codebook,
        decode_weight,
    )
    firsts = (
        heads_first,
        merge_first,
        expand_first,
        shrink_first,
        vectors_first,
        encode_first,
        codebook_first,
        decode_first,
    )
    seconds = (
        heads_second,
        merge_second,
        expand_second,
        shrink_second,
        vectors_second,
        encode_second,
        codebook_second,
        decode_second,
    )
    updates = [
        adam_update(
            masters[member],
            gradients[member] * factor,
            firsts[member],
            seconds[member],
            RATES[member],
            DECAYS[member],
        )
        for member in range(8)
    ]
    return (
        decoded_all,
        frame_grads,
        norm_before,
        updates[0][0],
        updates[0][1],
        updates[0][2],
        updates[0][3],
        updates[1][0],
        updates[1][1],
        updates[1][2],
        updates[1][3],
        updates[2][0],
        updates[2][1],
        updates[2][2],
        updates[2][3],
        updates[3][0],
        updates[3][1],
        updates[3][2],
        updates[3][3],
        updates[4][0],
        updates[4][1],
        updates[4][2],
        updates[4][3],
        updates[5][0],
        updates[5][1],
        updates[5][2],
        updates[5][3],
        updates[6][0],
        updates[6][1],
        updates[6][2],
        updates[6][3],
        updates[7][0],
        updates[7][1],
        updates[7][2],
        updates[7][3],
    )


def solution(mesh):
    return jax.shard_map(
        local,
        mesh=mesh,
        in_specs=(
            P("dp", "tensor", None),
            P("dp", "tensor"),
            P(),
            P("dp", "tensor", None),
            P(None, None, "dp", "tensor"),
            P(None, "tensor", "dp"),
            P(None, "dp", "tensor"),
            P(None, "tensor", "dp"),
            P(None, ("dp", "tensor")),
            P(("dp", "tensor"), None),
            P(("dp", "tensor"), None),
            P(None, ("dp", "tensor")),
            P(None, None, "dp", "tensor"),
            P(None, "tensor", "dp"),
            P(None, "dp", "tensor"),
            P(None, "tensor", "dp"),
            P(None, ("dp", "tensor")),
            P(("dp", "tensor"), None),
            P(("dp", "tensor"), None),
            P(None, ("dp", "tensor")),
            P(None, None, "dp", "tensor"),
            P(None, "tensor", "dp"),
            P(None, "dp", "tensor"),
            P(None, "tensor", "dp"),
            P(None, ("dp", "tensor")),
            P(("dp", "tensor"), None),
            P(("dp", "tensor"), None),
            P(None, ("dp", "tensor")),
        ),
        out_specs=(
            P("dp", "tensor", None),
            P("dp", "tensor", None),
            P(),
            P(None, None, "dp", "tensor"),
            P(None, None, "dp", "tensor"),
            P(None, None, "dp", "tensor"),
            P(None, None, "dp", "tensor"),
            P(None, "tensor", "dp"),
            P(None, "tensor", "dp"),
            P(None, "tensor", "dp"),
            P(None, "tensor", "dp"),
            P(None, "dp", "tensor"),
            P(None, "dp", "tensor"),
            P(None, "dp", "tensor"),
            P(None, "dp", "tensor"),
            P(None, "tensor", "dp"),
            P(None, "tensor", "dp"),
            P(None, "tensor", "dp"),
            P(None, "tensor", "dp"),
            P(None, ("dp", "tensor")),
            P(None, ("dp", "tensor")),
            P(None, ("dp", "tensor")),
            P(None, ("dp", "tensor")),
            P(("dp", "tensor"), None),
            P(("dp", "tensor"), None),
            P(("dp", "tensor"), None),
            P(("dp", "tensor"), None),
            P(("dp", "tensor"), None),
            P(("dp", "tensor"), None),
            P(("dp", "tensor"), None),
            P(("dp", "tensor"), None),
            P(None, ("dp", "tensor")),
            P(None, ("dp", "tensor")),
            P(None, ("dp", "tensor")),
            P(None, ("dp", "tensor")),
        ),
        check_vma=False,
    )
```

profile of v0, /device:TPU:0, one launch (start us, length us, event | category | flops | bytes accessed | tf_op | source)
XLA Modules:
  0.0 2142.3 jit_solution(1577431367146715066)
XLA Ops:
  13.4 70.7 %all_gather.80 = bf16[15,512]{0,1:T(8,128)(2,1)S(1)} all-gather(bf16[15,16]{0,1:T(8,128)(2,1)S(1)} %copy.217), channel_id=1, replica_groups=mesh['dp'=16,'tensor'=2] {'dp','tensor'}, dimensions={1}, use_global_device_ids=true | all-gather | bytes 15840 | tf_op jit(solution)/shard_map/all_gather | solution.py:307
  86.5 19.2 all_gather.82
  107.8 67.0 %all_gather.86 = bf16[8192,32]{0,1:T(8,128)(2,1)S(1)} all-gather(bf16[256,32]{0,1:T(8,128)(2,1)S(1)} %convert_element_type.466), channel_id=1, replica_groups=mesh['dp'=16,'tensor'=2] {'dp','tensor'}, dimensions={0}, use_global_device_ids=true | all-gather | bytes 540672 | tf_op jit(solution)/shard_map/all_gather | solution.py:309
  176.5 66.2 %all_gather.87 = bf16[32,512]{0,1:T(8,128)(2,1)S(1)} all-gather(bf16[32,16]{0,1:T(8,128)(2,1)S(1)} %convert_element_type.467), channel_id=1, replica_groups=mesh['dp'=16,'tensor'=2] {'dp','tensor'}, dimensions={1}, use_global_device_ids=true | all-gather | bytes 33792 | tf_op jit(solution)/shard_map/all_gather | solution.py:310
  243.5 68.9 %all_gather.85 = bf16[512,32]{1,0:T(8,128)(2,1)} all-gather(bf16[16,32]{1,0:T(8,128)(2,1)S(1)} %convert_element_type.465), channel_id=1, replica_groups=mesh['dp'=16,'tensor'=2] {'dp','tensor'}, dimensions={0}, use_global_device_ids=true | all-gather | bytes 33792 | tf_op jit(solution)/shard_map/all_gather | solution.py:308
  316.0 6.8 fusion.181
  339.9 928.0 %while.32 = (s32[]{:T(128)}, f32[2,3,512,256]{2,3,1,0:T(8,128)}, f32[2,256,512]{2,1,0:T(8,128)}, f32[2,512,1024]{2,1,0:T(8,128)}, f32[2,1024,512]{2,1,0:T(8,128)...) while((s32[]{:T(128)}, f32[2,3,512,256]{2,3,1,0:T(8,128)}, ...), condition=%wide.region_64.65_spmd.clone, body=%wide.region_3.64_spmd.clone.sunk | while | flops 26555596800 | bytes 1191722880 | solution.py:363
  347.5 19.4 all-gather.22.cloned.1.call-done
  384.1 18.8 reduce-scatter.35.cloned.1.call-done
  409.7 15.9 all-gather.30.cloned.1.call-done
  442.4 6.0 all-gather.24.cloned.1.call-done
  453.2 18.1 all-gather.26.cloned.1.call-done
  471.3 6.6 fusion.513
  487.1 6.8 reduce-scatter.41.cloned.1.call-done
  498.9 17.6 reduce-scatter.37.cloned.1.call-done
  516.5 22.6 %reduce-scatter.39.cloned.1.call-done = bf16[512,512]{0,1:T(8,128)(2,1)} async-done(((bf16[1024,512]{0,1:T(8,128)(2,1)}), bf16[512,512]{0,1:T(8,128)(2,1)}) %reduce-scatter.39.cloned.1.call-update) | async-done | bytes 524304 | tf_op jit(solution)/shard_map/while/body/eval_jaxpr/reduce_scatter | solution.py:135
  546.2 15.7 all-gather.32.cloned.1.call-done
  569.4 15.4 all-gather.28.cloned.1.call-done
  586.7 8.0 multiply_reduce_fusion.43
  629.8 13.8 reduce-scatter.45.cloned.1.call-done
  658.9 20.7 all-gather.34.cloned.1.call-done
  703.5 7.3 scatter_fusion
  729.9 12.0 all-gather.36.cloned.1.call-done
  808.8 21.4 all-gather.22.cloned.1.call-done
  847.3 18.8 reduce-scatter.35.cloned.1.call-done
  872.9 16.1 all-gather.30.cloned.1.call-done
  905.6 6.3 all-gather.24.cloned.1.call-done
  916.6 18.0 all-gather.26.cloned.1.call-done
  934.6 6.6 fusion.513
  950.4 6.8 reduce-scatter.41.cloned.1.call-done
  962.2 17.6 reduce-scatter.37.cloned.1.call-done
  979.7 22.4 %reduce-scatter.39.cloned.1.call-done = bf16[512,512]{0,1:T(8,128)(2,1)} async-done(((bf16[1024,512]{0,1:T(8,128)(2,1)}), bf16[512,512]{0,1:T(8,128)(2,1)}) %reduce-scatter.39.cloned.1.call-update) | async-done | bytes 524304 | tf_op jit(solution)/shard_map/while/body/eval_jaxpr/reduce_scatter | solution.py:135
  1009.5 15.6 all-gather.32.cloned.1.call-done
  1032.7 15.4 all-gather.28.cloned.1.call-done
  1049.9 8.0 multiply_reduce_fusion.43
  1093.1 13.8 reduce-scatter.45.cloned.1.call-done
  1122.1 20.7 all-gather.34.cloned.1.call-done
  1166.6 7.3 scatter_fusion
  1193.6 11.3 all-gather.36.cloned.1.call-done
  1289.5 115.1 %reduce-scatter.33.cloned.1.call-done = f32[16,15]{1,0:T(8,128)} async-done(((f32[512,15]{1,0:T(8,128)}), f32[16,15]{1,0:T(8,128)}) %reduce-scatter.33.cloned.1.call-update) | async-done | bytes 976
  1406.0 130.7 %reduce-scatter.27.cloned.1.call-done = f32[16,32]{1,0:T(8,128)} async-done(((f32[512,32]{1,0:T(8,128)}), f32[16,32]{1,0:T(8,128)}) %reduce-scatter.27.cloned.1.call-update) | async-done | bytes 2064 | tf_op jit(solution)/shard_map/reduce_scatter | solution.py:374
  1538.1 130.8 %reduce-scatter.31.cloned.1.call-done = f32[32,16]{0,1:T(8,128)} async-done(((f32[32,512]{0,1:T(8,128)}), f32[32,16]{0,1:T(8,128)}) %reduce-scatter.31.cloned.1.call-update) | async-done | bytes 2064 | tf_op jit(solution)/shard_map/reduce_scatter | solution.py:376
  1670.3 55.9 %reduce-scatter.21.cloned.1.call-done = f32[2,256,32]{1,2,0:T(8,128)} async-done(((f32[2,256,512]{1,2,0:T(8,128)}), f32[2,256,32]{1,2,0:T(8,128)}) %reduce-scatter.21.cloned.1.call-update) | async-done | bytes 65552 | tf_op jit(solution)/shard_map/reduce_scatter | solution.py:368
  1727.6 134.6 %reduce-scatter.29.cloned.1.call-done = f32[256,32]{0,1:T(8,128)} async-done(((f32[8192,32]{0,1:T(8,128)}), f32[256,32]{0,1:T(8,128)}) %reduce-scatter.29.cloned.1.call-update) | async-done | bytes 32784 | tf_op jit(solution)/shard_map/reduce_scatter | solution.py:375
  1863.7 65.0 %reduce-scatter.19.cloned.1.call-done = f32[2,3,32,256]{3,2,1,0:T(8,128)} async-done(((f32[2,3,512,256]{3,2,1,0:T(8,128)}), f32[2,3,32,256]{3,2,1,0:T(8,128)}) %reduce-scatter.19.cloned.1.call-update) | async-done | bytes 196624 | tf_op jit(solution)/shard_map/reduce_scatter | solution.py:367
  1931.6 72.9 %reduce-scatter.23.cloned.1.call-done = f32[2,32,1024]{2,1,0:T(8,128)} async-done(((f32[2,512,1024]{2,1,0:T(8,128)}), f32[2,32,1024]{2,1,0:T(8,128)}) %reduce-scatter.23.cloned.1.call-update) | async-done | bytes 262160 | tf_op jit(solution)/shard_map/reduce_scatter | solution.py:369
  2006.8 72.8 %reduce-scatter.25.cloned.1.call-done = f32[2,1024,32]{1,2,0:T(8,128)} async-done(((f32[2,1024,512]{1,2,0:T(8,128)}), f32[2,1024,32]{1,2,0:T(8,128)}) %reduce-scatter.25.cloned.1.call-update) | async-done | bytes 262160 | tf_op jit(solution)/shard_map/reduce_scatter | solution.py:370
  2084.5 39.7 %psum.7 = f32[]{:T(128)} all-reduce(f32[]{:T(128)S(6)} %add.808), channel_id=1, replica_groups=mesh['dp'=16,'tensor'=2] {'dp','tensor'}, use_global_device_ids=true, to_apply=%region_81.82 | all-reduce | flops 1 | bytes 8 | tf_op jit(solution)/shard_map/psum | solution.py:382
  (1200 shorter events, 542.6 us)
Async XLA Ops:
  7.2 306.1 %all-gather.16.cloned.1.call-start = ((), (), s32[]{:S(2)}) async-start(), calls=%async_computation.16 | async-start | bytes 1671168 | tf_op jit(solution)/shard_map/all_gather | solution.py:301
  8.9 307.1 %all-gather.20.cloned.1.call-start = ((), (), s32[]{:S(2)}) async-start(), calls=%async_computation.18 | async-start | bytes 2228224 | tf_op jit(solution)/shard_map/all_gather | solution.py:304
  10.8 323.6 %all-gather.18.cloned.1.call-start = ((), (), s32[]{:S(2)}) async-start(), calls=%async_computation.17 | async-start | bytes 2228224 | tf_op jit(solution)/shard_map/all_gather | solution.py:303
  340.1 26.8 %all-gather.22.cloned.1.call-start = ((), (), s32[]{:S(2)}) async-start(), calls=%async_computation.27 | async-start | bytes 1572864 | tf_op jit(solution)/shard_map/while/body/eval_jaxpr/all_gather | solution.py:52
  347.5 55.4 %reduce-scatter.35.cloned.1.call-start = ((), (), s32[]{:S(2)}) async-start(), calls=%async_computation.28 | async-start | bytes 1572864 | tf_op jit(solution)/shard_map/while/body/eval_jaxpr/reduce_scatter | solution.py:120
  382.3 43.2 %all-gather.30.cloned.1.call-start = ((), (), s32[]{:S(2)}) async-start(), calls=%async_computation.34 | async-start | bytes 1572864 | tf_op jit(solution)/shard_map/while/body/eval_jaxpr/all_gather | solution.py:52
  384.0 64.4 %all-gather.24.cloned.1.call-start = ((), (), s32[]{:S(2)}) async-start(), calls=%async_computation.29 | async-start | bytes 1572864 | tf_op jit(solution)/shard_map/while/body/eval_jaxpr/all_gather | solution.py:52
  405.3 66.0 %all-gather.26.cloned.1.call-start = ((), (), s32[]{:S(2)}) async-start(), calls=%async_computation.30 | async-start | bytes 1572864 | tf_op jit(solution)/shard_map/while/body/eval_jaxpr/all_gather | solution.py:56
  409.4 84.6 %reduce-scatter.41.cloned.1.call-start = ((), (), s32[]{:S(2)}) async-start(), calls=%async_computation.35 | async-start | bytes 1572864 | tf_op jit(solution)/shard_map/while/body/eval_jaxpr/reduce_scatter | solution.py:120
  441.9 74.6 %reduce-scatter.37.cloned.1.call-start = ((), (), s32[]{:S(2)}) async-start(), calls=%async_computation.31 | async-start | bytes 1572864 | tf_op jit(solution)/shard_map/while/body/eval_jaxpr/reduce_scatter | solution.py:183
  481.6 57.4 %reduce-scatter.39.cloned.1.call-start = ((), (), s32[]{:S(2)}) async-start(), calls=%async_computation.32 | async-start | bytes 1572864 | tf_op jit(solution)/shard_map/while/body/eval_jaxpr/reduce_scatter | solution.py:135
  487.0 74.9 %all-gather.32.cloned.1.call-start = ((), (), s32[]{:S(2)}) async-start(), calls=%async_computation.36 | async-start | bytes 1572864 | tf_op jit(solution)/shard_map/while/body/eval_jaxpr/all_gather | solution.py:52
  498.8 86.0 %all-gather.28.cloned.1.call-start = ((), (), s32[]{:S(2)}) async-start(), calls=%async_computation.33 | async-start | bytes 1572864 | tf_op jit(solution)/shard_map/while/body/eval_jaxpr/all_gather | solution.py:56
  545.9 78.8 %reduce-scatter.43.cloned.1.call-start = ((), (), s32[]{:S(2)}) async-start(), calls=%async_computation.37 | async-start | bytes 1572864 | tf_op jit(solution)/shard_map/while/body/eval_jaxpr/reduce_scatter | solution.py:135
  569.4 74.3 %reduce-scatter.45.cloned.1.call-start = ((), (), s32[]{:S(2)}) async-start(), calls=%async_computation.38 | async-start | bytes 1572864 | tf_op jit(solution)/shard_map/while/body/eval_jaxpr/reduce_scatter | solution.py:201
  623.2 56.4 %all-gather.34.cloned.1.call-start = ((), (), s32[]{:S(2)}) async-start(), calls=%async_computation.39 | async-start | bytes 1572864 | tf_op jit(solution)/shard_map/while/body/eval_jaxpr/all_gather | solution.py:56
  658.1 52.7 %reduce-scatter.47.cloned.1.call-start = ((), (), s32[]{:S(2)}) async-start(), calls=%async_computation.40 | async-start | bytes 1572864 | tf_op jit(solution)/shard_map/while/body/eval_jaxpr/reduce_scatter | solution.py:183
  688.9 53.0 %all-gather.36.cloned.1.call-start = ((), (), s32[]{:S(2)}) async-start(), calls=%async_computation.41 | async-start | bytes 1572864 | tf_op jit(solution)/shard_map/while/body/eval_jaxpr/all_gather | solution.py:56
  720.4 74.7 %reduce-scatter.49.cloned.1.call-start = ((), (), s32[]{:S(2)}) async-start(), calls=%async_computation.42 | async-start | bytes 1572864 | tf_op jit(solution)/shard_map/while/body/eval_jaxpr/reduce_scatter | solution.py:201
  801.3 28.8 %all-gather.22.cloned.1.call-start = ((), (), s32[]{:S(2)}) async-start(), calls=%async_computation.27 | async-start | bytes 1572864 | tf_op jit(solution)/shard_map/while/body/eval_jaxpr/all_gather | solution.py:52
  808.7 57.4 %reduce-scatter.35.cloned.1.call-start = ((), (), s32[]{:S(2)}) async-start(), calls=%async_computation.28 | async-start | bytes 1572864 | tf_op jit(solution)/shard_map/while/body/eval_jaxpr/reduce_scatter | solution.py:120
  845.6 43.4 %all-gather.30.cloned.1.call-start = ((), (), s32[]{:S(2)}) async-start(), calls=%async_computation.34 | async-start | bytes 1572864 | tf_op jit(solution)/shard_map/while/body/eval_jaxpr/all_gather | solution.py:52
  847.3 64.6 %all-gather.24.cloned.1.call-start = ((), (), s32[]{:S(2)}) async-start(), calls=%async_computation.29 | async-start | bytes 1572864 | tf_op jit(solution)/shard_map/while/body/eval_jaxpr/all_gather | solution.py:52
  868.6 66.0 %all-gather.26.cloned.1.call-start = ((), (), s32[]{:S(2)}) async-start(), calls=%async_computation.30 | async-start | bytes 1572864 | tf_op jit(solution)/shard_map/while/body/eval_jaxpr/all_gather | solution.py:56
  872.6 84.6 %reduce-scatter.41.cloned.1.call-start = ((), (), s32[]{:S(2)}) async-start(), calls=%async_computation.35 | async-start | bytes 1572864 | tf_op jit(solution)/shard_map/while/body/eval_jaxpr/reduce_scatter | solution.py:120
  905.3 74.4 %reduce-scatter.37.cloned.1.call-start = ((), (), s32[]{:S(2)}) async-start(), calls=%async_computation.31 | async-start | bytes 1572864 | tf_op jit(solution)/shard_map/while/body/eval_jaxpr/reduce_scatter | solution.py:183
  944.9 57.3 %reduce-scatter.39.cloned.1.call-start = ((), (), s32[]{:S(2)}) async-start(), calls=%async_computation.32 | async-start | bytes 1572864 | tf_op jit(solution)/shard_map/while/body/eval_jaxpr/reduce_scatter | solution.py:135
  950.3 74.9 %all-gather.32.cloned.1.call-start = ((), (), s32[]{:S(2)}) async-start(), calls=%async_computation.36 | async-start | bytes 1572864 | tf_op jit(solution)/shard_map/while/body/eval_jaxpr/all_gather | solution.py:52
  962.1 86.0 %all-gather.28.cloned.1.call-start = ((), (), s32[]{:S(2)}) async-start(), calls=%async_computation.33 | async-start | bytes 1572864 | tf_op jit(solution)/shard_map/while/body/eval_jaxpr/all_gather | solution.py:56
  1009.1 78.9 %reduce-scatter.43.cloned.1.call-start = ((), (), s32[]{:S(2)}) async-start(), calls=%async_computation.37 | async-start | bytes 1572864 | tf_op jit(solution)/shard_map/while/body/eval_jaxpr/reduce_scatter | solution.py:135
  1032.7 74.2 %reduce-scatter.45.cloned.1.call-start = ((), (), s32[]{:S(2)}) async-start(), calls=%async_computation.38 | async-start | bytes 1572864 | tf_op jit(solution)/shard_map/while/body/eval_jaxpr/reduce_scatter | solution.py:201
  1086.5 56.4 %all-gather.34.cloned.1.call-start = ((), (), s32[]{:S(2)}) async-start(), calls=%async_computation.39 | async-start | bytes 1572864 | tf_op jit(solution)/shard_map/while/body/eval_jaxpr/all_gather | solution.py:56
  1121.3 52.5 %reduce-scatter.47.cloned.1.call-start = ((), (), s32[]{:S(2)}) async-start(), calls=%async_computation.40 | async-start | bytes 1572864 | tf_op jit(solution)/shard_map/while/body/eval_jaxpr/reduce_scatter | solution.py:183
  1152.1 52.8 %all-gather.36.cloned.1.call-start = ((), (), s32[]{:S(2)}) async-start(), calls=%async_computation.41 | async-start | bytes 1572864 | tf_op jit(solution)/shard_map/while/body/eval_jaxpr/all_gather | solution.py:56
  1183.5 74.7 %reduce-scatter.49.cloned.1.call-start = ((), (), s32[]{:S(2)}) async-start(), calls=%async_computation.42 | async-start | bytes 1572864 | tf_op jit(solution)/shard_map/while/body/eval_jaxpr/reduce_scatter | solution.py:201
  1267.8 136.8 %reduce-scatter.33.cloned.1.call-start = ((), (), s32[]{:S(2)}) async-start(), calls=%async_computation.26 | async-start | bytes 270336
  1269.5 267.2 %reduce-scatter.27.cloned.1.call-start = ((), (), s32[]{:S(2)}) async-start(), calls=%async_computation.23 | async-start | bytes 270336 | tf_op jit(solution)/shard_map/reduce_scatter | solution.py:374
  1271.3 397.6 %reduce-scatter.31.cloned.1.call-start = ((), (), s32[]{:S(2)}) async-start(), calls=%async_computation.25 | async-start | bytes 270336 | tf_op jit(solution)/shard_map/reduce_scatter | solution.py:376
  1273.0 453.1 %reduce-scatter.21.cloned.1.call-start = ((), (), s32[]{:S(2)}) async-start(), calls=%async_computation.20 | async-start | bytes 1114112 | tf_op jit(solution)/shard_map/reduce_scatter | solution.py:368
  1275.7 586.5 %reduce-scatter.29.cloned.1.call-start = ((), (), s32[]{:S(2)}) async-start(), calls=%async_computation.24 | async-start | bytes 1081344 | tf_op jit(solution)/shard_map/reduce_scatter | solution.py:375
  1279.4 649.4 %reduce-scatter.19.cloned.1.call-start = ((), (), s32[]{:S(2)}) async-start(), calls=%async_computation.19 | async-start | bytes 3342336 | tf_op jit(solution)/shard_map/reduce_scatter | solution.py:367
  1283.0 721.5 %reduce-scatter.23.cloned.1.call-start = ((), (), s32[]{:S(2)}) async-start(), calls=%async_computation.21 | async-start | bytes 4456448 | tf_op jit(solution)/shard_map/reduce_scatter | solution.py:369
  1283.7 795.9 %reduce-scatter.25.cloned.1.call-start = ((), (), s32[]{:S(2)}) async-start(), calls=%async_computation.22 | async-start | bytes 4456448 | tf_op jit(solution)/shard_map/reduce_scatter | solution.py:370
  1289.4 843.3 %copy-start.166 = (f32[256,32]{0,1:T(8,128)S(1)}, f32[256,32]{0,1:T(8,128)}, u32[]{:S(2)}) copy-start(f32[256,32]{0,1:T(8,128)} %param.40) | copy-start | bytes 98308
  1289.4 843.3 %copy-start.170 = (f32[256,32]{0,1:T(8,128)S(1)}, f32[256,32]{0,1:T(8,128)}, u32[]{:S(2)}) copy-start(f32[256,32]{0,1:T(8,128)} %param.56) | copy-start | bytes 98308
  1289.4 844.0 %copy-start.176 = (f32[32,16]{0,1:T(8,128)S(1)}, f32[32,16]{0,1:T(8,128)}, u32[]{:S(2)}) copy-start(f32[32,16]{0,1:T(8,128)} %param.41) | copy-start | bytes 6148
  1289.5 844.0 %copy-start.183 = (f32[32,16]{0,1:T(8,128)S(1)}, f32[32,16]{0,1:T(8,128)}, u32[]{:S(2)}) copy-start(f32[32,16]{0,1:T(8,128)} %param.57) | copy-start | bytes 6148
  1289.5 844.0 %copy-start.184 = (f32[32,16]{0,1:T(8,128)S(1)}, f32[32,16]{0,1:T(8,128)}, u32[]{:S(2)}) copy-start(f32[32,16]{0,1:T(8,128)} %param.49) | copy-start | bytes 6148
  (370 other events, 22871.1 us)
Sparse Core Ops, SparseCore 0:
  10.8 42.5 all-gather.15
  56.2 41.3 all-gather.19
  100.4 40.7 all-gather.17
  347.6 19.2 all-gather.21
  382.5 20.3 reduce-scatter.34
  404.2 21.2 all-gather.29
  427.1 21.2 all-gather.23
  450.0 21.2 all-gather.25
  473.6 20.3 reduce-scatter.40
  496.1 20.3 reduce-scatter.36
  518.7 20.3 reduce-scatter.38
  540.5 21.2 all-gather.31
  563.5 21.2 all-gather.27
  587.0 20.3 reduce-scatter.42
  623.3 20.3 reduce-scatter.44
  658.2 21.2 all-gather.33
  689.0 20.3 reduce-scatter.46
  720.5 21.2 all-gather.35
  774.8 20.3 reduce-scatter.48
  808.8 21.2 all-gather.21
  845.7 20.3 reduce-scatter.34
  867.6 21.2 all-gather.29
  890.5 21.2 all-gather.23
  913.3 21.2 all-gather.25
  936.8 20.3 reduce-scatter.40
  959.4 20.3 reduce-scatter.36
  981.8 20.3 reduce-scatter.38
  1003.8 21.2 all-gather.31
  1026.8 21.2 all-gather.27
  1050.3 20.3 reduce-scatter.42
  1086.6 20.2 reduce-scatter.44
  1121.5 21.3 all-gather.33
  1152.2 20.3 reduce-scatter.46
  1183.6 21.2 all-gather.35
  1237.8 20.3 reduce-scatter.48
  1271.2 133.3 reduce-scatter.32
  1407.4 129.3 reduce-scatter.26
  1539.5 129.3 reduce-scatter.30
  1672.8 53.3 reduce-scatter.20
  1728.4 133.7 reduce-scatter.28
  1866.5 62.1 reduce-scatter.18
  1933.1 71.3 reduce-scatter.22
  2008.2 71.3 reduce-scatter.24
where the time goes:
time: 2150 us; the launch traced here: 2140 us
  waiting for transfers between devices  1190 us (55%)
  blocking collectives  332 us (15%)
  matrix products  272 us (13%)
  other arithmetic  190 us (9%)
  local copies, waits for them, and re-layouts  122 us (6%)
  between operations  22 us (1%)
    dot_general x100, matrix products, fast_dot(): jnp.einsum(formula, first_arg, second_arg, preferred_element_type=jnp.flo...  258 us
    reduce_scatter x1, waiting for transfers between devices, local(): lax.psum_scatter(small_acc[2], ('dp', 'tensor'), scatter_dimension=0, til...  135 us
    all_gather x8, waiting for transfers between devices, gather_cotangent(): lax.all_gather(local_rows.astype(jnp.bfloat16), 'tensor', axis=0, tiled=T...  132 us
    reduce_scatter x1, waiting for transfers between devices, local(): lax.psum_scatter(small_acc[3], ('dp', 'tensor'), scatter_dimension=1, til...  131 us
    reduce_scatter x1, waiting for transfers between devices, local(): lax.psum_scatter(small_acc[1], ('dp', 'tensor'), scatter_dimension=0, til...  131 us
    all_gather x8, waiting for transfers between devices, gather_tensor(): return lax.all_gather(local_rows, 'tensor', axis=0, tiled=True)  116 us
    unnamed x12, waiting for transfers between devices  116 us
    reduce_scatter x1, waiting for transfers between devices, local(): lax.psum_scatter(block_acc[2], 'dp', scatter_dimension=1, tiled=True)  72.9 us
  transfers between devices with their start and end apart: 43, of which 36 were waited for; matrix products, arithmetic and copies ran while one was open for 16% of the time, Pallas kernels for 0%

commit v1 on v0

--- a/solution.py
+++ b/solution.py
@@ -46,14 +46,6 @@
         precision=lax.Precision.HIGHEST,
         preferred_element_type=jnp.float32,
     )
-
-
-def gather_tensor(local_rows):
-    return lax.all_gather(local_rows, "tensor", axis=0, tiled=True)
-
-
-def gather_cotangent(local_rows):
-    return lax.all_gather(local_rows.astype(jnp.bfloat16), "tensor", axis=0, tiled=True)
 
 
 def attend_forward(projected, block_rows):
@@ -112,44 +104,19 @@
 
 def block_forward(token_rows, weight_set, vector_rows, block_rows):
     head_proj, merge_proj, expand_proj, shrink_proj = weight_set
-    rows_here = token_rows.shape[0]
     normed = layer_norm(token_rows, vector_rows[0], vector_rows[1]).astype(jnp.bfloat16)
-    normed_all = gather_tensor(normed)
-    projected = fast_dot("td,cde->cte", normed_all, head_proj).astype(jnp.bfloat16)
+    projected = fast_dot("td,cde->cte", normed, head_proj).astype(jnp.bfloat16)
     mixture, log_sums = attend_forward(projected, block_rows)
-    merged = lax.psum_scatter(
-        fast_dot(
-            "te,ed->td",
-            lax.slice_in_dim(mixture, 0, rows_here * lax.axis_size("tensor"), axis=0),
-            merge_proj,
-        ).astype(jnp.bfloat16),
-        "tensor",
-        scatter_dimension=0,
-        tiled=True,
-    ).astype(jnp.float32)
-    hidden = token_rows + merged + vector_rows[2]
+    hidden = token_rows + fast_dot("te,de->td", mixture, merge_proj) + vector_rows[2]
     normed_mlp = layer_norm(hidden, vector_rows[3], vector_rows[4]).astype(jnp.bfloat16)
-    normed_mlp_all = gather_tensor(normed_mlp)
-    expanded = fast_dot("td,df->tf", normed_mlp_all, expand_proj)
+    expanded = fast_dot("td,df->tf", normed_mlp, expand_proj)
     active = gelu_tanh(expanded).astype(jnp.bfloat16)
-    shrunk = lax.psum_scatter(
-        fast_dot(
-            "tf,fd->td",
-            lax.slice_in_dim(active, 0, rows_here * lax.axis_size("tensor"), axis=0),
-            shrink_proj,
-        ).astype(jnp.bfloat16),
-        "tensor",
-        scatter_dimension=0,
-        tiled=True,
-    ).astype(jnp.float32)
-    output = hidden + shrunk + vector_rows[5]
+    output = hidden + fast_dot("tf,df->td", active, shrink_proj) + vector_rows[5]
     kept_values = (
         token_rows,
         hidden,
         normed,
         normed_mlp,
-        normed_all,
-        normed_mlp_all,
         projected,
         mixture,
         log_sums,
@@ -166,48 +133,27 @@
         hidden,
         normed,
         normed_mlp,
-        normed_all,
-        normed_mlp_all,
         projected,
         mixture,
         log_sums,
         expanded,
         active,
     ) = kept_values
-    rows_here = grad_out.shape[0]
-    dshrink_all = gather_cotangent(grad_out)
-    dshrink = fast_dot("tf,td->fd", active, dshrink_all)
-    dactive = fast_dot("td,fd->tf", dshrink_all, shrink_proj)
+    grad_low = grad_out.astype(jnp.bfloat16)
+    dshrink = fast_dot("td,tf->df", grad_low, active)
+    dactive = fast_dot("td,df->tf", grad_low, shrink_proj)
     dexpanded = jax.vjp(gelu_tanh, expanded)[1](dactive)[0].astype(jnp.bfloat16)
-    dexpand = fast_dot("td,tf->df", normed_mlp_all, dexpanded)
-    dnormed_mlp = lax.psum_scatter(
-        fast_dot(
-            "tf,df->td",
-            lax.slice_in_dim(dexpanded, 0, rows_here * lax.axis_size("tensor"), axis=0),
-            expand_proj,
-        ).astype(jnp.bfloat16),
-        "tensor",
-        scatter_dimension=0,
-        tiled=True,
-    ).astype(jnp.float32)
+    dexpand = fast_dot("td,tf->df", normed_mlp, dexpanded)
+    dnormed_mlp = fast_dot("tf,df->td", dexpanded, expand_proj)
     pullback_mlp = jax.vjp(layer_norm, hidden, vector_rows[3], vector_rows[4])[1]
     dhidden_norm, gain_grad_mlp, shift_grad_mlp = pullback_mlp(dnormed_mlp)
     dhidden = grad_out + dhidden_norm
-    dmerge_all = gather_cotangent(dhidden)
-    dmerge = fast_dot("te,td->ed", mixture, dmerge_all)
-    dmixture = fast_dot("td,ed->te", dmerge_all, merge_proj).astype(jnp.bfloat16)
+    dhidden_low = dhidden.astype(jnp.bfloat16)
+    dmerge = fast_dot("td,te->de", dhidden_low, mixture)
+    dmixture = fast_dot("td,de->te", dhidden_low, merge_proj).astype(jnp.bfloat16)
     dprojected = attend_backward(projected, log_sums, dmixture, block_rows)
-    dheads = fast_dot("td,cte->cde", normed_all, dprojected)
-    dnormed = lax.psum_scatter(
-        fast_dot(
-            "cte,cde->td",
-            lax.slice_in_dim(dprojected, 0, rows_here * lax.axis_size("tensor"), axis=1),
-            head_proj,
-        ).astype(jnp.bfloat16),
-        "tensor",
-        scatter_dimension=0,
-        tiled=True,
-    ).astype(jnp.float32)
+    dheads = fast_dot("td,cte->cde", normed, dprojected)
+    dnormed = fast_dot("cte,cde->td", dprojected, head_proj)
     pullback_attn = jax.vjp(layer_norm, token_rows, vector_rows[0], vector_rows[1])[1]
     dtoken_norm, gain_grad, shift_grad = pullback_attn(dnormed)
     dvectors = jnp.stack(
@@ -253,6 +199,76 @@
         dencoded,
         (jnp.stack([gain_grad, shift_grad, dstart_bias]), dencode, dcodebook, ddecode),
     )
+
+
+def pack_shard(heads, merge, expand, shrink):
+    parts = [heads[0], heads[1], heads[2], merge.T, expand, shrink.T]
+    return jnp.concatenate([part.astype(jnp.bfloat16) for part in parts], axis=1)
+
+
+def unpack_shard(rows):
+    width = rows.shape[1] // 12
+    heads = jnp.stack([rows[:, 0:width], rows[:, width : 2 * width], rows[:, 2 * width : 3 * width]])
+    merge = rows[:, 3 * width : 4 * width].T
+    expand = rows[:, 4 * width : 8 * width]
+    shrink = rows[:, 8 * width : 12 * width].T
+    return (heads, merge, expand, shrink)
+
+
+def gather_block(rows):
+    gathered = lax.all_gather(rows, ("dp", "tensor"), axis=0, tiled=False)
+    split = gathered.reshape(lax.axis_size("dp"), 2, rows.shape[0], rows.shape[1])
+    return split.transpose(1, 0, 2, 3).reshape(2, -1, rows.shape[1])
+
+
+def weight_views(packed):
+    width = packed.shape[2] // 12
+
+    def join(first, last):
+        return jnp.concatenate([packed[0, :, first:last], packed[1, :, first:last]], axis=1)
+
+    heads = jnp.stack([join(part * width, (part + 1) * width) for part in range(3)])
+    merge = join(3 * width, 4 * width)
+    expand = join(4 * width, 8 * width)
+    shrink = join(8 * width, 12 * width)
+    return (heads, merge, expand, shrink)
+
+
+def pack_grads(heads, merge, expand, shrink):
+    def halves(array):
+        half = array.shape[1] // 2
+        return jnp.stack([array[:, :half], array[:, half:]])
+
+    parts = [halves(part) for part in (heads[0], heads[1], heads[2], merge, expand, shrink)]
+    return jnp.concatenate(parts, axis=2).astype(jnp.bfloat16)
+
+
+def reduce_block(packed):
+    dp_size = lax.axis_size("dp")
+    split = packed.reshape(2, dp_size, -1, packed.shape[2]).transpose(1, 0, 2, 3)
+    split = split.reshape(-1, packed.shape[2])
+    return lax.psum_scatter(split, ("dp", "tensor"), scatter_dimension=0, tiled=True).astype(jnp.float32)
+
+
+def swap_half(rows):
+    return lax.ppermute(rows, "tensor", [(0, 1), (1, 0)])
+
+
+def pick_frame(pair, index):
+    return lax.dynamic_index_in_dim(pair, index, axis=0, keepdims=False)
+
+
+def join_frame(pair):
+    mine = lax.axis_index("tensor")
+    return jnp.concatenate([pick_frame(pair, mine), swap_half(pick_frame(pair, 1 - mine))], axis=0)
+
+
+def split_frame(rows):
+    mine = lax.axis_index("tensor")
+    half = rows.shape[0] // 2
+    other = swap_half(rows[half:].astype(jnp.bfloat16)).astype(jnp.float32)
+    own = rows[:half]
+    return jnp.where(mine == 0, jnp.stack([own, other]), jnp.stack([other, own]))
 
 
 def adam_update(master, gradient, first_state, second_state, step_rate, decay_rate):
@@ -297,84 +313,73 @@
     codebook_second,
     decode_second,
 ):
-    block_low = (
-        lax.all_gather(heads_weight.astype(jnp.bfloat16), "dp", axis=2, tiled=True),
-        lax.all_gather(merge_weight.astype(jnp.bfloat16), "dp", axis=2, tiled=True),
-        lax.all_gather(expand_weight.astype(jnp.bfloat16), "dp", axis=1, tiled=True),
-        lax.all_gather(shrink_weight.astype(jnp.bfloat16), "dp", axis=2, tiled=True),
-    )
-    small_low = (
-        lax.all_gather(vectors.astype(jnp.bfloat16), ("dp", "tensor"), axis=1, tiled=True),
-        lax.all_gather(encode_weight.astype(jnp.bfloat16), ("dp", "tensor"), axis=0, tiled=True),
-        lax.all_gather(codebook.astype(jnp.bfloat16), ("dp", "tensor"), axis=0, tiled=True),
-        lax.all_gather(decode_weight.astype(jnp.bfloat16), ("dp", "tensor"), axis=1, tiled=True),
-    )
+    own_rows = [
+        pack_shard(heads_weight[b], merge_weight[b], expand_weight[b], shrink_weight[b])
+        for b in range(2)
+    ]
+    small_parts = [vectors, encode_weight, codebook, decode_weight]
+    small_flat = jnp.concatenate([part.astype(jnp.bfloat16).reshape(-1) for part in small_parts])
+    small_all = lax.all_gather(small_flat, ("dp", "tensor"), axis=0, tiled=False)
+    small_low = []
+    offset = 0
+    for part, cut_dim in zip(small_parts, (1, 0, 0, 1)):
+        piece = small_all[:, offset : offset + part.size].reshape((-1,) + part.shape)
+        offset += part.size
+        if cut_dim == 1:
+            piece = piece.transpose(1, 0, 2).reshape(part.shape[0], -1)
+        else:
+            piece = piece.reshape(-1, part.shape[1])
+        small_low.append(piece)
     vector_set = small_low[0].astype(jnp.float32)
     small_set = (vector_set, small_low[1], small_low[2], small_low[3])
-    micro_count = frames.shape[0]
-    frame_len = frames.shape[1] * lax.axis_size("tensor")
-    block_rows = min(512, frame_len)
+    frame_rows = join_frame(frames).astype(jnp.float32)
+    code_ids = join_frame(codes)
+    cotangent = join_frame(out_cotangent).astype(jnp.float32)
+    weight_sets = [weight_views(gather_block(rows)) for rows in own_rows]
+    block_rows = frame_rows.shape[0] // 2
+    frame_id = lax.axis_index("dp") * frames.shape[0] + lax.axis_index("tensor")
     clip_ends = jnp.cumsum(clip_frames)
-    frame_ids = lax.axis_index("dp") * micro_count + jnp.arange(micro_count, dtype=jnp.int32)
-    clip_ids = jnp.sum((clip_ends[None, :] <= frame_ids[:, None]).astype(jnp.int32), axis=1)
+    clip_id = jnp.sum((clip_ends <= frame_id).astype(jnp.int32))
     clip_slots = jnp.arange(clip_frames.shape[0], dtype=jnp.int32)
-    clip_counts = jnp.sum(
-        jnp.where(clip_slots[None, :] == clip_ids[:, None], clip_frames[None, :], 0), axis=1
-    )
-    clip_weights = 1.0 / clip_counts.astype(jnp.float32)
-    encoder_set = tuple((gathered[0] for gathered in block_low))
-    decoder_set = tuple((gathered[1] for gathered in block_low))
-    block_init = tuple((jnp.zeros(gathered.shape, jnp.float32) for gathered in block_low))
-    small_init = tuple((jnp.zeros(gathered.shape, jnp.float32) for gathered in small_low))
-
-    def one_micro(carried, inputs):
-        block_acc, small_acc = carried
-        frame_rows, code_ids, cotangent, clip_weight = inputs
-        encoded, kept_encoder = block_forward(
-            frame_rows.astype(jnp.float32), encoder_set, vector_set[0:6], block_rows
-        )
-        started, kept_quant = quantize_forward(encoded, code_ids, small_set)
-        decoded, kept_decoder = block_forward(started, decoder_set, vector_set[6:12], block_rows)
-        dstarted, decoder_grads, decoder_vectors = block_backward(
-            kept_decoder, cotangent.astype(jnp.float32), decoder_set, vector_set[6:12], block_rows
-        )
-        dencoded, quant_grads = quantize_backward(
-            kept_quant, dstarted, code_ids, clip_weight, small_set
-        )
-        dframe, encoder_grads, encoder_vectors = block_backward(
-            kept_encoder, dencoded, encoder_set, vector_set[0:6], block_rows
-        )
-        block_new = tuple(
-            (
-                jnp.stack([first_part, second_part])
-                for first_part, second_part in zip(encoder_grads, decoder_grads)
-            )
-        )
-        small_new = (
-            jnp.concatenate([encoder_vectors, decoder_vectors, quant_grads[0]], axis=0),
-            quant_grads[1],
-            quant_grads[2],
-            quant_grads[3],
-        )
-        block_acc = tuple((running + addition for running, addition in zip(block_acc, block_new)))
-        small_acc = tuple((running + addition for running, addition in zip(small_acc, small_new)))
-        return ((block_acc, small_acc), (decoded, dframe))
-
-    (block_acc, small_acc), (decoded_all, frame_grads) = lax.scan(
-        one_micro, (block_init, small_init), (frames, codes, out_cotangent, clip_weights)
-    )
-    block_grads = (
-        lax.psum_scatter(block_acc[0], "dp", scatter_dimension=2, tiled=True),
-        lax.psum_scatter(block_acc[1], "dp", scatter_dimension=2, tiled=True),
-        lax.psum_scatter(block_acc[2], "dp", scatter_dimension=1, tiled=True),
-        lax.psum_scatter(block_acc[3], "dp", scatter_dimension=2, tiled=True),
-    )
-    small_grads = (
-        lax.psum_scatter(small_acc[0], ("dp", "tensor"), scatter_dimension=1, tiled=True),
-        lax.psum_scatter(small_acc[1], ("dp", "tensor"), scatter_dimension=0, tiled=True),
-        lax.psum_scatter(small_acc[2], ("dp", "tensor"), scatter_dimension=0, tiled=True),
-        lax.psum_scatter(small_acc[3], ("dp", "tensor"), scatter_dimension=1, tiled=True),
-    )
+    clip_count = jnp.sum(jnp.where(clip_slots == clip_id, clip_frames, 0))
+    clip_weight = 1.0 / clip_count.astype(jnp.float32)
+    encoded, kept_encoder = block_forward(
+        frame_rows, weight_sets[0], vector_set[0:6], block_rows
+    )
+    started, kept_quant = quantize_forward(encoded, code_ids, small_set)
+    decoded, kept_decoder = block_forward(started, weight_sets[1], vector_set[6:12], block_rows)
+    dstarted, decoder_grads, decoder_vectors = block_backward(
+        kept_decoder, cotangent, weight_sets[1], vector_set[6:12], block_rows
+    )
+    dencoded, quant_grads = quantize_backward(
+        kept_quant, dstarted, code_ids, clip_weight, small_set
+    )
+    dframe, encoder_grads, encoder_vectors = block_backward(
+        kept_encoder, dencoded, weight_sets[0], vector_set[0:6], block_rows
+    )
+    decoded_all = split_frame(decoded)
+    frame_grads = split_frame(dframe)
+    reduced = [
+        unpack_shard(reduce_block(pack_grads(*grads))) for grads in (encoder_grads, decoder_grads)
+    ]
+    block_grads = [jnp.stack([first, second]) for first, second in zip(*reduced)]
+    device_count = lax.axis_size("dp") * lax.axis_size("tensor")
+    dvectors = jnp.concatenate([encoder_vectors, decoder_vectors, quant_grads[0]], axis=0)
+    small_new = (dvectors, quant_grads[1], quant_grads[2], quant_grads[3])
+    columns = []
+    for gradient, part, cut_dim in zip(small_new, small_parts, (1, 0, 0, 1)):
+        if cut_dim == 1:
+            gradient = gradient.reshape(part.shape[0], device_count, -1).transpose(1, 0, 2)
+        columns.append(gradient.reshape(device_count, -1))
+    small_sum = lax.psum_scatter(
+        jnp.concatenate(columns, axis=1), ("dp", "tensor"), scatter_dimension=0, tiled=True
+    )
+    small_sum = small_sum.reshape(-1)
+    small_grads = []
+    offset = 0
+    for part in small_parts:
+        small_grads.append(small_sum[offset : offset + part.size].reshape(part.shape))
+        offset += part.size
     gradients = tuple(block_grads) + tuple(small_grads)
     local_squares = jnp.zeros((), jnp.float32)
     for gradient in gradients:

time: 2150 us -> 1100 us (0.51)
  waiting for transfers between devices: 1190 us -> 481 us
  blocking collectives: 332 us -> 40.1 us
  other arithmetic: 190 us -> 131 us
  local copies, waits for them, and re-layouts: 122 us -> 148 us
    reduce_scatter x23 -> x2, waiting for transfers between devices: 825 us -> 235 us  [reduce_block(): lax.psum_scatter(split, ('dp', 'tensor'), scatter_dimension=0, tiled=True)]
    all_gather x5 -> x0, blocking collectives: 292 us -> none  [the longest x1 70.7 us: local(): lax.all_gather(vectors.astype(jnp.bfloat16), ('dp', 'tensor'), axis=1, ti...]
    all_gather x19 -> x2, waiting for transfers between devices: 248 us -> 51.1 us  [gather_block(): gathered = lax.all_gather(rows, ('dp', 'tensor'), axis=0, tiled=False)]
    unnamed x12 -> x8, waiting for transfers between devices: 116 us -> 181 us
    while x690 -> x0, local copies, waits for them, and re-layouts: 61.9 us -> none
    unnamed x78 -> x579, local copies, waits for them, and re-layouts: 22.2 us -> 60.5 us
    dot_general x100 -> x50, matrix products: 258 us -> 251 us  [fast_dot(): jnp.einsum(formula, first_arg, second_arg, preferred_element_type=jnp.flo...]
  transfers between devices with their start and end apart: 43 -> 11, of which waited for: 36 -> 7; matrix products, arithmetic and copies ran while one was open for 16% -> 19% of each run, Pallas kernels for 0% -> 0%
where the time goes in v1:
time: 1100 us; the launch traced here: 1090 us
  waiting for transfers between devices  481 us (44%)
  matrix products  259 us (24%)
  local copies, waits for them, and re-layouts  148 us (13%)
  other arithmetic  131 us (12%)
  blocking collectives  40.1 us (4%)
  between operations  25.7 us (2%)
    dot_general x50, matrix products, fast_dot(): jnp.einsum(formula, first_arg, second_arg, preferred_element_type=jnp.flo...  251 us
    reduce_scatter x2, waiting for transfers between devices, reduce_block(): lax.psum_scatter(split, ('dp', 'tensor'), scatter_dimension=0, tiled=True)  235 us
    unnamed x8, waiting for transfers between devices  181 us
    unnamed x579, local copies, waits for them, and re-layouts  60.5 us
    all_gather x2, waiting for transfers between devices, gather_block(): gathered = lax.all_gather(rows, ('dp', 'tensor'), axis=0, tiled=False)  51.1 us
    psum x1, blocking collectives, local(): norm_before = jnp.sqrt(lax.psum(local_squares, ('dp', 'tensor')))  40.1 us
    convert_element_type x4, other arithmetic, attend_backward(): dscores = (attend * (dattend - inner_sum)).astype(jnp.bfloat16)  38.9 us
  transfers between devices with their start and end apart: 11, of which 7 were waited for; matrix products, arithmetic and copies ran while one was open for 19% of the time, Pallas kernels for 0%

profile of v1, /device:TPU:0, one launch (start us, length us, event | category | flops | bytes accessed | tf_op | source)
XLA Modules:
  0.0 1091.8 jit_solution(6464580135732279536)
XLA Ops:
  28.3 115.6 %all-reduce.5.cloned.1.call-done = bf16[302592]{0:T(1024)(128)(2,1)} async-done(((bf16[302592]{0:T(1024)(128)(2,1)}), bf16[302592]{0:T(1024)(128)(2,1)}) %all-reduce.5.cloned.1.call-update) | async-done | bytes 605200
  166.5 51.1 %all-gather.6.cloned.1.call-done = bf16[1024,3072]{1,0:T(8,128)(2,1)} async-done(((bf16[32,3072]{1,0:T(8,128)(2,1)}), bf16[1024,3072]{1,0:T(8,128)(2,1)}) %all-gather.6.cloned.1.call-update) | async-done | bytes 6291472 | tf_op jit(solution)/shard_map/all_gather | solution.py:219
  237.4 8.7 multiply_reduce_fusion.6
  246.1 3.8 fusion
  250.0 4.3 fusion.71
  254.3 8.0 fusion.1
  265.2 4.3 fusion.70
  275.4 9.3 fusion.22
  284.6 4.3 fusion.195
  291.8 3.6 multiply_reduce_fusion.10
  300.3 15.1 %multiply_reduce_fusion.1 = (f32[8,512]{1,0:T(8,128)}, f32[8,512,1024]{2,1,0:T(8,128)}) fusion(f32[8,512,1024]{2,1,0:T(8,128)} %copy-done.2, f32[8,512]{1,0:T(8,128)S(1)} %log_add_fusion.1, bf16[512,8,64]{0,2,1:T(8,128)(2,1)} %bitcast.401, bf16[1024,8,64]{0,2,1:T(8,128)(2,1)} %bitcast.385), kind=kOutput, calls=%fused_computation.6 | convolution fusion | flops 553644032 | bytes 35160064 | tf_op jit(solution)/shard_map/qhd,khd->hqk/dot_general | solution.py:38
  317.2 8.0 multiply_convert_fusion.1
  331.5 7.6 fusion.73
  339.1 9.2 fusion.8
  348.3 10.2 multiply_reduce_fusion
  383.8 8.1 multiply_convert_fusion
  399.2 6.8 multiply_convert_fusion.6
  408.3 10.6 add_convert_fusion
  421.2 6.0 fusion.194
  437.1 3.4 fusion.2
  443.0 5.1 fusion.69
  450.6 3.4 fusion.3
  456.4 5.0 fusion.68
  468.4 3.5 fusion.191
  492.9 9.5 fusion.29
  502.4 4.3 fusion.193
  517.6 15.1 %multiply_reduce_fusion.3 = (f32[8,512]{1,0:T(8,128)}, f32[8,512,1024]{2,1,0:T(8,128)}) fusion(f32[8,512,1024]{2,1,0:T(8,128)} %copy-done, f32[8,512]{1,0:T(8,128)S(1)} %log_add_fusion.3, bf16[512,8,64]{0,2,1:T(8,128)(2,1)S(1)} %bitcast.403, bf16[1024,8,64]{0,2,1:T(8,128)(2,1)} %bitcast.379), kind=kOutput, calls=%fused_computation.12 | convolution fusion | flops 553644032 | bytes 35160064 | tf_op jit(solution)/shard_map/qhd,khd->hqk/dot_general | solution.py:38
  534.5 10.9 multiply_convert_fusion.3
  545.3 7.0 fusion.75
  555.3 14.1 %multiply_reduce_fusion.2 = (f32[8,512]{1,0:T(8,128)}, f32[8,512,1024]{2,1,0:T(8,128)}) fusion(f32[8,512,1024]{2,1,0:T(8,128)} %copy-done.1, f32[8,512]{1,0:T(8,128)} %log_add_fusion.2, bf16[512,8,64]{0,2,1:T(8,128)(2,1)S(1)} %bitcast.407, bf16[1024,8,64]{0,2,1:T(8,128)(2,1)} %bitcast.380), kind=kOutput, calls=%fused_computation.9 | convolution fusion | flops 553644032 | bytes 35160064 | tf_op jit(solution)/shard_map/qhd,khd->hqk/dot_general | solution.py:38
  569.4 5.2 fusion.12
  576.4 8.3 convolution_convert_fusion.2
  584.7 3.8 convolution_convert_fusion.3
  590.4 8.4 scatter_custom_fusion
  598.9 4.5 reshape.701
  603.6 12.0 %multiply_convert_fusion.2 = bf16[8,512,1024]{2,1,0:T(8,128)(2,1)S(1)} fusion(f32[8,512,1024]{2,1,0:T(8,128)} %get-tuple-element.410, f32[8,512,1024]{2,1,0:T(8,128)} %copy-done.1, f32[8,512]{1,0:T(8,128)S(1)} %copy-done.145, f32[8,512]{1,0:T(8,128)S(1)} %copy-done.117), kind=kLoop, calls=%fused_computation.8 | loop fusion | flops 20971520 | bytes 41975808 | tf_op jit(solution)/shard_map/convert_element_type | solution.py:91
  621.0 5.2 multiply_convert_fusion.7
  628.1 9.1 add_convert_fusion.1
  639.1 4.8 fusion.192
  664.5 3.9 convolution_bitcast_fusion
  676.0 4.8 convolution_convert_fusion
  690.2 6.8 add_add_fusion.9
  698.7 4.8 collective-permute-done.3
  705.7 9.0 collective-permute-done.1
  716.1 65.4 %all-reduce.7.cloned.1.call-done = f32[32,9456]{1,0:T(8,128)} async-done(((f32[32,9456]{1,0:T(8,128)}), f32[32,9456]{1,0:T(8,128)}) %all-reduce.7.cloned.1.call-update) | async-done | bytes 1210384
  785.9 116.5 %reduce-scatter.3.cloned.1.call-done = bf16[32,3072]{1,0:T(8,128)(2,1)} async-done(((bf16[1024,3072]{1,0:T(8,128)(2,1)}), bf16[32,3072]{1,0:T(8,128)(2,1)}) %reduce-scatter.3.cloned.1.call-update) | async-done | bytes 196624 | tf_op jit(solution)/shard_map/reduce_scatter | solution.py:250
  903.4 118.0 %reduce-scatter.5.cloned.1.call-done = bf16[32,3072]{1,0:T(8,128)(2,1)} async-done(((bf16[1024,3072]{1,0:T(8,128)(2,1)}), bf16[32,3072]{1,0:T(8,128)(2,1)}) %reduce-scatter.5.cloned.1.call-update) | async-done | bytes 196624 | tf_op jit(solution)/shard_map/reduce_scatter | solution.py:250
  1032.1 40.1 %psum.7 = f32[]{:T(128)} all-reduce(f32[]{:T(128)S(6)} %add.539), channel_id=1, replica_groups=mesh['dp'=16,'tensor'=2] {'dp','tensor'}, use_global_device_ids=true, to_apply=%region_66.67 | all-reduce | flops 1 | bytes 8 | tf_op jit(solution)/shard_map/psum | solution.py:387
  (874 shorter events, 259.7 us)
Async XLA Ops:
  7.3 136.7 %all-reduce.5.cloned.1.call-start = ((), (), s32[]{:S(2)}) async-start(), calls=%async_computation.6 | async-start | bytes 1212416
  12.4 205.2 %all-gather.6.cloned.1.call-start = ((), (), s32[]{:S(2)}) async-start(), calls=%async_computation.4 | async-start | bytes 6488064 | tf_op jit(solution)/shard_map/all_gather | solution.py:219
  15.0 343.4 %all-gather.8.cloned.1.call-start = ((), (), s32[]{:S(2)}) async-start(), calls=%async_computation.5 | async-start | bytes 6488064 | tf_op jit(solution)/shard_map/all_gather | solution.py:219
  15.1 12.5 %collective-permute-start = (s32[512]{0:T(512)S(1)}, s32[512]{0:T(512)S(1)}, u32[]{:S(2)}, u32[]{:S(2)}) collective-permute-start(s32[512]{0:T(512)S(1)} %bitcast.470), channel_id=1, source_target_pairs={{0,1},{1,0},{2,3},{3,2},{4,5},{5,4},{6,7},{7,6},{8,9},{9,8},{10,11... | collective-permute-start | bytes 6152 | tf_op jit(solution)/shard_map/ppermute | solution.py:254
  20.5 254.8 %collective-permute-start.4 = (bf16[512,512]{0,1:T(8,128)(2,1)}, bf16[512,512]{0,1:T(8,128)(2,1)}, u32[]{:S(2)}, u32[]{:S(2)}) collective-permute-start(bf16[512,512]{0,1:T(8,128)(2,1)} %bitcast.126), channel_id=1, source_target_pairs={{0,1},{1,0},{2,3},{3,2},{4,5},{5,4},{6,7},{7,6},{8,9},{9,8},{10,11... | collective-permute-start | bytes 1572872 | tf_op jit(solution)/shard_map/ppermute | solution.py:254
  21.6 143.4 %collective-permute-start.2 = (bf16[512,512]{0,1:T(8,128)(2,1)}, bf16[512,512]{0,1:T(8,128)(2,1)S(1)}, u32[]{:S(2)}, u32[]{:S(2)}) collective-permute-start(bf16[512,512]{0,1:T(8,128)(2,1)} %bitcast.52), channel_id=1, source_target_pairs={{0,1},{1,0},{2,3},{3,2},{4,5},{5,4},{6,7},{7,6},{8,9},{9,8},{10,11... | collective-permute-start | bytes 1572872 | tf_op jit(solution)/shard_map/ppermute | solution.py:254
  23.6 757.9 %all-reduce.7.cloned.1.call-start = ((), (), s32[]{:S(2)}) async-start(), calls=%async_computation.7 | async-start | bytes 2424832
  27.0 138.6 %copy-start.39 = (bf16[1,512,512]{1,2,0:T(8,128)(2,1)}, bf16[1,512,512]{1,2,0:T(8,128)(2,1)S(1)}, u32[]{:S(2)}) copy-start(bf16[1,512,512]{1,2,0:T(8,128)(2,1)S(1)} %copy.376) | copy-start | bytes 1572868
  27.7 127.3 %copy-start.146 = (pred[1024]{0:T(1024)(128)(4,1)}, pred[1024]{0:T(1024)(128)(4,1)S(1)}, u32[]{:S(2)}) copy-start(pred[1024]{0:T(1024)(128)(4,1)S(1)} %compare_and_fusion) | copy-start | bytes 3076
  154.6 277.8 %copy-start.141 = (f32[512]{0:T(512)}, f32[512]{0:T(512)S(1)}, u32[]{:S(2)}) copy-start(f32[512]{0:T(512)S(1)} %add.472) | copy-start | bytes 6148
  155.5 318.1 %copy-start.8 = (f32[1024,512]{0,1:T(8,128)}, f32[1024,512]{0,1:T(8,128)S(1)}, u32[]{:S(2)}) copy-start(f32[1024,512]{0,1:T(8,128)S(1)} %get-tuple-element.385) | copy-start | bytes 6291460
  155.5 74.9 %copy-start.138 = (f32[1024]{0:T(1024)}, f32[1024]{0:T(1024)S(1)}, u32[]{:S(2)}) copy-start(f32[1024]{0:T(1024)S(1)} %broadcast_multiply_fusion.4) | copy-start | bytes 12292
  155.8 74.7 %copy-start.189 = (f32[512]{0:T(512)}, f32[512]{0:T(512)S(1)}, u32[]{:S(2)}) copy-start(f32[512]{0:T(512)S(1)} %mul.876) | copy-start | bytes 6148
  157.7 137.7 %copy-start.197 = (f32[512]{0:T(512)}, f32[512]{0:T(512)S(1)}, u32[]{:S(2)}) copy-start(f32[512]{0:T(512)S(1)} %mul.884) | copy-start | bytes 6148
  157.9 112.8 %copy-start.221 = (f32[512]{0:T(512)}, f32[512]{0:T(512)S(1)}, u32[]{:S(2)}) copy-start(f32[512]{0:T(512)S(1)} %add.484) | copy-start | bytes 6148
  165.0 65.5 %copy-start.155 = (f32[1024]{0:T(1024)}, f32[1024]{0:T(1024)S(1)}, u32[]{:S(2)}) copy-start(f32[1024]{0:T(1024)S(1)} %fusion.110) | copy-start | bytes 12292
  165.0 55.8 %copy-start.43 = (bf16[512,512]{0,1:T(8,128)(2,1)}, bf16[512,512]{0,1:T(8,128)(2,1)S(1)}, u32[]{:S(2)}) copy-start(bf16[512,512]{0,1:T(8,128)(2,1)S(1)} %collective-permute-done.2) | copy-start | bytes 1572868
  165.6 55.2 %copy-start.135 = (f32[1024]{0:T(1024)}, f32[1024]{0:T(1024)S(1)}, u32[]{:S(2)}) copy-start(f32[1024]{0:T(1024)S(1)} %broadcast_multiply_fusion.2) | copy-start | bytes 12292
  165.9 54.9 %copy-start.162 = (f32[1024]{0:T(1024)}, f32[1024]{0:T(1024)S(1)}, u32[]{:S(2)}) copy-start(f32[1024]{0:T(1024)S(1)} %fusion.51) | copy-start | bytes 12292
  232.8 29.6 %copy-start.48 = (bf16[1,1024,512]{1,2,0:T(8,128)(2,1)}, bf16[1,1024,512]{1,2,0:T(8,128)(2,1)S(1)}, u32[]{:S(2)}) copy-start(bf16[1,1024,512]{1,2,0:T(8,128)(2,1)S(1)} %get-tuple-element.301) | copy-start | bytes 3145732
  234.9 40.4 %copy-start.93 = (bf16[512,1024]{1,0:T(8,128)(2,1)}, bf16[512,1024]{1,0:T(8,128)(2,1)S(1)}, u32[]{:S(2)}) copy-start(bf16[512,1024]{1,0:T(8,128)(2,1)S(1)} %get-tuple-element.282) | copy-start | bytes 3145732
  234.9 40.4 %copy-start.95 = (bf16[512,1024]{1,0:T(8,128)(2,1)}, bf16[512,1024]{1,0:T(8,128)(2,1)S(1)}, u32[]{:S(2)}) copy-start(bf16[512,1024]{1,0:T(8,128)(2,1)S(1)} %get-tuple-element.283) | copy-start | bytes 3145732
  254.3 15.2 %copy-start.236 = (bf16[8,64,512]{2,1,0:T(8,128)(2,1)}, bf16[8,64,512]{2,1,0:T(8,128)(2,1)S(1)}, u32[]{:S(2)}) copy-start(bf16[8,64,512]{2,1,0:T(8,128)(2,1)S(1)} %fusion.71) | copy-start | bytes 1572868
  270.4 25.0 %copy-start.151 = (f32[1024]{0:T(1024)}, f32[1024]{0:T(1024)S(1)}, u32[]{:S(2)}) copy-start(f32[1024]{0:T(1024)S(1)} %broadcast_multiply_fusion.3) | copy-start | bytes 12292
  270.7 24.7 %copy-start.168 = (f32[1024]{0:T(1024)}, f32[1024]{0:T(1024)S(1)}, u32[]{:S(2)}) copy-start(f32[1024]{0:T(1024)S(1)} %fusion.111) | copy-start | bytes 12292
  300.3 15.7 %slice-start.10 = ((s8[16777216]{0:T(1024)(128)(4,1)}), s8[4194304]{0:T(1024)(128)(4,1)S(1)}, s32[]{:S(2)}) async-start(s8[16777216]{0:T(1024)(128)(4,1)} %bitcast.347), calls=%async_computation.18 | async-start | bytes 8388608
  300.3 16.9 %slice-start.11 = ((s8[16777216]{0:T(1024)(128)(4,1)}), s8[4194304]{0:T(1024)(128)(4,1)S(1)}, s32[]{:S(2)}) async-start(s8[16777216]{0:T(1024)(128)(4,1)} %bitcast.347), calls=%async_computation.19 | async-start | bytes 8388608
  328.5 19.7 %slice-start.12 = ((s8[16777216]{0:T(1024)(128)(4,1)}), s8[4194304]{0:T(1024)(128)(4,1)S(1)}, s32[]{:S(2)}) async-start(s8[16777216]{0:T(1024)(128)(4,1)} %bitcast.349), calls=%async_computation.20 | async-start | bytes 8388608
  328.5 19.7 %slice-start.13 = ((s8[16777216]{0:T(1024)(128)(4,1)}), s8[4194304]{0:T(1024)(128)(4,1)S(1)}, s32[]{:S(2)}) async-start(s8[16777216]{0:T(1024)(128)(4,1)} %bitcast.349), calls=%async_computation.21 | async-start | bytes 8388608
  331.5 16.7 %slice-start.14 = ((s8[16777216]{0:T(1024)(128)(4,1)}), s8[4194304]{0:T(1024)(128)(4,1)S(1)}, s32[]{:S(2)}) async-start(s8[16777216]{0:T(1024)(128)(4,1)} %bitcast.349), calls=%async_computation.22 | async-start | bytes 8388608
  378.5 69.6 %copy-start.53 = (bf16[1,512,512]{1,2,0:T(8,128)(2,1)}, bf16[1,512,512]{1,2,0:T(8,128)(2,1)S(1)}, u32[]{:S(2)}) copy-start(bf16[1,512,512]{1,2,0:T(8,128)(2,1)S(1)} %get-tuple-element.295) | copy-start | bytes 1572868
  463.7 49.7 %copy-start.160 = (f32[1024]{0:T(1024)}, f32[1024]{0:T(1024)S(1)}, u32[]{:S(2)}) copy-start(f32[1024]{0:T(1024)S(1)} %fusion.113) | copy-start | bytes 12292
  491.9 21.6 %copy-start.200 = (f32[1024]{0:T(1024)}, f32[1024]{0:T(1024)S(1)}, u32[]{:S(2)}) copy-start(f32[1024]{0:T(1024)S(1)} %negate_multiply_fusion.4) | copy-start | bytes 12292
  515.9 72.7 %copy-start.10 = (f32[1024,512]{0,1:T(8,128)}, f32[1024,512]{0,1:T(8,128)S(1)}, u32[]{:S(2)}) copy-start(f32[1024,512]{0,1:T(8,128)S(1)} %get-tuple-element.263) | copy-start | bytes 6291460
  517.5 15.1 %slice-start.1 = ((s8[16777216]{0:T(1024)(128)(4,1)}), s8[4194304]{0:T(1024)(128)(4,1)S(1)}, s32[]{:S(2)}) async-start(s8[16777216]{0:T(1024)(128)(4,1)} %bitcast.343), calls=%async_computation.9 | async-start | bytes 8388608
  517.5 15.7 %slice-start.2 = ((s8[16777216]{0:T(1024)(128)(4,1)}), s8[4194304]{0:T(1024)(128)(4,1)S(1)}, s32[]{:S(2)}) async-start(s8[16777216]{0:T(1024)(128)(4,1)} %bitcast.343), calls=%async_computation.10 | async-start | bytes 8388608
  517.5 16.9 %slice-start.3 = ((s8[16777216]{0:T(1024)(128)(4,1)}), s8[4194304]{0:T(1024)(128)(4,1)S(1)}, s32[]{:S(2)}) async-start(s8[16777216]{0:T(1024)(128)(4,1)} %bitcast.343), calls=%async_computation.11 | async-start | bytes 8388608
  552.3 17.1 %slice-start.4 = ((s8[16777216]{0:T(1024)(128)(4,1)}), s8[4194304]{0:T(1024)(128)(4,1)S(1)}, s32[]{:S(2)}) async-start(s8[16777216]{0:T(1024)(128)(4,1)} %bitcast.345), calls=%async_computation.12 | async-start | bytes 8388608
  552.3 17.1 %slice-start.5 = ((s8[16777216]{0:T(1024)(128)(4,1)}), s8[4194304]{0:T(1024)(128)(4,1)S(1)}, s32[]{:S(2)}) async-start(s8[16777216]{0:T(1024)(128)(4,1)} %bitcast.345), calls=%async_computation.13 | async-start | bytes 8388608
  652.6 249.8 %reduce-scatter.3.cloned.1.call-start = ((), (), s32[]{:S(2)}) async-start(), calls=%async_computation.2 | async-start | bytes 6488064 | tf_op jit(solution)/shard_map/reduce_scatter | solution.py:250
  662.9 358.5 %reduce-scatter.5.cloned.1.call-start = ((), (), s32[]{:S(2)}) async-start(), calls=%async_computation.3 | async-start | bytes 6488064 | tf_op jit(solution)/shard_map/reduce_scatter | solution.py:250
  688.7 14.8 %collective-permute-start.3 = (bf16[512,512]{0,1:T(8,128)(2,1)S(1)}, bf16[512,512]{0,1:T(8,128)(2,1)S(1)}, u32[]{:S(2)}, u32[]{:S(2)}) collective-permute-start(bf16[512,512]{0,1:T(8,128)(2,1)S(1)} %slice.806), channel_id=1, source_target_pairs={{0,1},{1,0},{2,3},{3,2},{4,5},{5,4},{6,7},{7,6},{8,9},{9,8},{10,11... | collective-permute-start | bytes 1572872 | tf_op jit(solution)/shard_map/ppermute | solution.py:254
  697.9 16.8 %collective-permute-start.1 = (bf16[512,512]{0,1:T(8,128)(2,1)}, bf16[512,512]{0,1:T(8,128)(2,1)}, u32[]{:S(2)}, u32[]{:S(2)}) collective-permute-start(bf16[512,512]{0,1:T(8,128)(2,1)} %slice.807), channel_id=1, source_target_pairs={{0,1},{1,0},{2,3},{3,2},{4,5},{5,4},{6,7},{7,6},{8,9},{9,8},{10,11... | collective-permute-start | bytes 1572872 | tf_op jit(solution)/shard_map/ppermute | solution.py:254
  1030.2 45.8 %copy-start.83 = (f32[2,1024,32]{1,2,0:T(8,128)S(1)}, f32[2,1024,32]{1,2,0:T(8,128)}, u32[]{:S(2)}) copy-start(f32[2,1024,32]{1,2,0:T(8,128)} %param.35) | copy-start | bytes 786436
  1030.3 45.8 %copy-start.120 = (f32[2,1024,32]{1,2,0:T(8,128)S(1)}, f32[2,1024,32]{1,2,0:T(8,128)}, u32[]{:S(2)}) copy-start(f32[2,1024,32]{1,2,0:T(8,128)} %param.51) | copy-start | bytes 786436
  1032.1 46.1 %copy-start.85 = (f32[2,32,1024]{2,1,0:T(8,128)S(1)}, f32[2,32,1024]{2,1,0:T(8,128)}, u32[]{:S(2)}) copy-start(f32[2,32,1024]{2,1,0:T(8,128)} %param.34) | copy-start | bytes 786436
  1032.1 46.1 %copy-start.121 = (f32[2,32,1024]{2,1,0:T(8,128)S(1)}, f32[2,32,1024]{2,1,0:T(8,128)}, u32[]{:S(2)}) copy-start(f32[2,32,1024]{2,1,0:T(8,128)} %param.50) | copy-start | bytes 786436
  1032.1 46.1 %copy-start.122 = (f32[2,32,1024]{2,1,0:T(8,128)S(1)}, f32[2,32,1024]{2,1,0:T(8,128)}, u32[]{:S(2)}) copy-start(f32[2,32,1024]{2,1,0:T(8,128)} %param.42) | copy-start | bytes 786436
  (235 other events, 942.7 us)
Sparse Core Ops, SparseCore 0:
  13.9 129.9 all-reduce.4
  147.8 69.6 all-gather.5
  221.4 68.0 all-gather.7
  652.7 128.7 all-reduce.6
  787.9 114.4 reduce-scatter.2
  907.9 113.4 reduce-scatter.4

commit v2 on v1

--- a/solution.py
+++ b/solution.py
@@ -1,6 +1,10 @@
+import functools
+
 import jax
 import jax.numpy as jnp
 from jax import lax
+from jax.experimental import pallas as pl
+from jax.experimental.pallas import tpu as pltpu
 from jax.sharding import PartitionSpec as P
 
 HEAD_DIM = 64
@@ -201,37 +205,316 @@
     )
 
 
+MESH = pl.DeviceIdType.MESH
+
+
+def remote(src, dst, sems, slot, target):
+    send, recv = sems
+    return pltpu.make_async_remote_copy(
+        src_ref=src,
+        dst_ref=dst,
+        send_sem=send.at[slot],
+        recv_sem=recv.at[slot],
+        device_id=target,
+        device_id_type=MESH,
+    )
+
+
+def coordinates():
+    dp_index = lax.axis_index("dp")
+    y = lax.axis_index("tensor")
+    return dp_index // 4, (dp_index // 2) % 2, dp_index % 2, y
+
+
+def partners(z, x, c, y):
+    along_z = [(((z + step) % 4) * 4 + x * 2 + c, y) for step in (1, 2, 3)]
+    along_x = (z * 4 + (1 - x) * 2 + c, y)
+    along_y = (z * 4 + x * 2 + c, 1 - y)
+    along_core = (z * 4 + x * 2 + (1 - c), y)
+    return along_z, along_x, along_y, along_core
+
+
+def greet(targets):
+    barrier = pltpu.get_barrier_semaphore()
+    for target in targets:
+        pl.semaphore_signal(barrier, inc=1, device_id=target, device_id_type=MESH)
+    pl.semaphore_wait(barrier, len(targets))
+
+
+def gather_kernel(count, orders, *refs):
+    shards = refs[:count]
+    frames, cotangent, codes = refs[count : count + 3]
+    outs = refs[count + 3 : 2 * count + 3]
+    frame_out, cotangent_out, codes_out = refs[2 * count + 3 : 2 * count + 6]
+    local_sems, send_sems, recv_sems, swap_send, swap_recv = refs[2 * count + 6 :]
+    z, x, c, y = coordinates()
+    along_z, along_x, along_y, along_core = partners(z, x, c, y)
+    greet(along_z + [along_x, along_y, along_core])
+    sems, swaps = (send_sems, recv_sems), (swap_send, swap_recv)
+    pending = []
+    for slot, (source, target) in enumerate(
+        ((codes, codes_out), (frames, frame_out), (cotangent, cotangent_out))
+    ):
+        copy = remote(source.at[1 - y], target, swaps, slot, along_y)
+        pending.append(copy)
+        copy.start()
+    first, second, third, to_core = [], [], [], []
+    own = []
+    for i in range(count):
+        slot = outs[i].at[y, z, x, c]
+        copy = pltpu.make_async_copy(shards[i], slot, local_sems.at[i])
+        copy.start()
+        own.append(copy)
+        first.append([remote(shards[i], slot, sems, (i, k), along_z[k]) for k in range(3)])
+        for copy in first[i]:
+            copy.start()
+        by_x = orders[i] == "xy"
+        column = outs[i].at[y, :, x, c]
+        second.append(remote(column, column, sems, (i, 3), along_x if by_x else along_y))
+        plane = outs[i].at[y, :, :, c] if by_x else outs[i].at[:, :, x, c]
+        third.append(remote(plane, plane, sems, (i, 4), along_y if by_x else along_x))
+        got_second = outs[i].at[y, :, 1 - x, c] if by_x else outs[i].at[1 - y, :, x, c]
+        got_third = outs[i].at[1 - y, :, :, c] if by_x else outs[i].at[:, :, 1 - x, c]
+        to_core.append(
+            [
+                remote(part, part, sems, (i, 5 + k), along_core)
+                for k, part in enumerate((column, got_second, got_third))
+            ]
+        )
+    for step in range(count + 2):
+        i = step
+        if i < count:
+            own[i].wait()
+            for copy in first[i]:
+                copy.wait_recv()
+            second[i].start()
+            to_core[i][0].start()
+        i = step - 1
+        if 0 <= i < count:
+            second[i].wait_recv()
+            third[i].start()
+            to_core[i][1].start()
+        i = step - 2
+        if 0 <= i < count:
+            third[i].wait_recv()
+            to_core[i][2].start()
+    for i in range(count):
+        for copy in first[i] + [second[i], third[i]]:
+            copy.wait_send()
+        for copy in to_core[i]:
+            copy.wait()
+    for copy in pending:
+        copy.wait()
+
+
+ORDERS = ("xy", "yx", "xy", "yx", "xy", "yx", "yx")
+
+
+def gather_tuned(shards, frames, cotangent, codes):
+    count = len(shards)
+    any_spec = pl.BlockSpec(memory_space=pl.ANY)
+    outs = [jax.ShapeDtypeStruct((2, 4, 2, 2) + s.shape, s.dtype) for s in shards]
+    outs += [jax.ShapeDtypeStruct(a.shape[1:], a.dtype) for a in (frames, cotangent, codes)]
+    results = pl.pallas_call(
+        functools.partial(gather_kernel, count, ORDERS),
+        out_shape=outs,
+        in_specs=[any_spec] * (count + 3),
+        out_specs=[any_spec] * (count + 3),
+        scratch_shapes=[
+            pltpu.SemaphoreType.DMA((count,)),
+            pltpu.SemaphoreType.DMA((count, 8)),
+            pltpu.SemaphoreType.DMA((count, 8)),
+            pltpu.SemaphoreType.DMA((3,)),
+            pltpu.SemaphoreType.DMA((3,)),
+        ],
+        compiler_params=pltpu.CompilerParams(collective_id=0, has_side_effects=True),
+        name="gather",
+    )(*shards, frames, cotangent, codes)
+    full = [r.reshape(2, 16 * r.shape[4], r.shape[5]) for r in results[:count]]
+    return full, results[count], results[count + 1], results[count + 2]
+
+
+def reduce_kernel(count, orders, *refs):
+    partial = refs[:count]
+    outs = refs[count : 2 * count]
+    total_out = refs[2 * count]
+    scratch = refs[2 * count + 1 :]
+    held = scratch[:count]
+    from_core = scratch[count : 2 * count]
+    from_third = scratch[2 * count : 3 * count]
+    from_second = scratch[3 * count : 4 * count]
+    from_first = scratch[4 * count : 5 * count]
+    squares, local_sems, send_sems, recv_sems, sum_send, sum_recv = scratch[5 * count :]
+    z, x, c, y = coordinates()
+    along_z, along_x, along_y, along_core = partners(z, x, c, y)
+    greet(along_z + [along_x, along_y, along_core])
+    sems = (send_sems, recv_sems)
+    own, core, third, second, first = [], [], [], [], []
+    for i in range(count):
+        by_x = orders[i] == "xy"
+        copy = remote(partial[i].at[:, :, :, 1 - c], from_core[i], sems, (i, 0), along_core)
+        copy.start()
+        core.append(copy)
+        copy = pltpu.make_async_copy(partial[i].at[:, :, :, c], held[i], local_sems.at[i])
+        copy.start()
+        own.append(copy)
+        if by_x:
+            third.append(remote(held[i].at[1 - y], from_third[i], sems, (i, 1), along_y))
+            second.append(remote(held[i].at[y, :, 1 - x], from_second[i], sems, (i, 2), along_x))
+        else:
+            third.append(remote(held[i].at[:, :, 1 - x], from_third[i], sems, (i, 1), along_x))
+            second.append(remote(held[i].at[1 - y, :, x], from_second[i], sems, (i, 2), along_y))
+        first.append(
+            [
+                remote(
+                    held[i].at[y, (z + k + 1) % 4, x],
+                    from_first[i].at[k],
+                    sems,
+                    (i, 3 + k),
+                    along_z[k],
+                )
+                for k in range(3)
+            ]
+        )
+
+    def add(into, index, other, other_index):
+        total = into[index].astype(jnp.float32) + other[other_index].astype(jnp.float32)
+        into[index] = total.astype(jnp.bfloat16)
+
+    for step in range(count + 3):
+        i = step
+        if i < count:
+            core[i].wait_recv()
+            own[i].wait()
+
+            @pl.loop(0, 16)
+            def _(n, i=i):
+                a, b, d = n // 8, (n // 2) % 4, n % 2
+                add(held[i], (a, b, d), from_core[i], (a, b, d))
+
+            third[i].start()
+        i = step - 1
+        if 0 <= i < count:
+            third[i].wait_recv()
+            by_x = orders[i] == "xy"
+
+            @pl.loop(0, 8)
+            def _(n, i=i, by_x=by_x):
+                if by_x:
+                    a, b = n // 2, n % 2
+                    add(held[i], (y, a, b), from_third[i], (a, b))
+                else:
+                    a, b = n // 4, n % 4
+                    add(held[i], (a, b, x), from_third[i], (a, b))
+
+            second[i].start()
+        i = step - 2
+        if 0 <= i < count:
+            second[i].wait_recv()
+            for k in range(4):
+                add(held[i], (y, k, x), from_second[i], (k,))
+            for copy in first[i]:
+                copy.start()
+        i = step - 3
+        if 0 <= i < count:
+            total = held[i][y, z, x].astype(jnp.float32)
+            for k in range(3):
+                first[i][k].wait_recv()
+                total = total + from_first[i][k].astype(jnp.float32)
+            outs[i][...] = total
+    square = jnp.zeros((8, 128), jnp.float32)
+    for i in range(count):
+        whole = outs[i][...]
+        rows, width = whole.shape
+        whole = whole * whole
+        for r in range(0, rows, 8):
+            for w in range(0, width, 128):
+                square = square + whole[r : r + 8, w : w + 128]
+    square = jnp.broadcast_to(jnp.sum(square, keepdims=True), (8, 128))
+    squares[0] = square
+    sums = (sum_send, sum_recv)
+    stage = 0
+    for n, targets in enumerate(([along_core], [along_x], [along_y], along_z)):
+        copies = []
+        for k, target in enumerate(targets):
+            copy = remote(squares.at[n], squares.at[4 + stage], sums, stage, target)
+            copy.start()
+            copies.append((copy, 4 + stage))
+            stage += 1
+        total = squares[n]
+        for copy, place in copies:
+            copy.wait()
+            total = total + squares[place]
+        if n < 3:
+            squares[n + 1] = total
+    total_out[...] = total
+    for i in range(count):
+        core[i].wait_send()
+        third[i].wait_send()
+        second[i].wait_send()
+        for copy in first[i]:
+            copy.wait_send()
+
+
+def reduce_tuned(partials):
+    count = len(partials)
+    rows = [p.shape[1] // 16 for p in partials]
+    widths = [p.shape[2] for p in partials]
+    split = [p.reshape(2, 4, 2, 2, r, w) for p, r, w in zip(partials, rows, widths)]
+    any_spec = pl.BlockSpec(memory_space=pl.ANY)
+    vmem = pl.BlockSpec(memory_space=pltpu.VMEM)
+    sizes = list(zip(rows, widths))
+    scratch = [pltpu.VMEM((2, 4, 2) + s, jnp.bfloat16) for s in sizes] * 2
+    scratch += [
+        pltpu.VMEM(((4, 2) if ORDERS[i] == "xy" else (2, 4)) + s, jnp.bfloat16)
+        for i, s in enumerate(sizes)
+    ]
+    scratch += [pltpu.VMEM((4,) + s, jnp.bfloat16) for s in sizes]
+    scratch += [pltpu.VMEM((3,) + s, jnp.bfloat16) for s in sizes]
+    scratch += [
+        pltpu.VMEM((10, 8, 128), jnp.float32),
+        pltpu.SemaphoreType.DMA((count,)),
+        pltpu.SemaphoreType.DMA((count, 6)),
+        pltpu.SemaphoreType.DMA((count, 6)),
+        pltpu.SemaphoreType.DMA((6,)),
+        pltpu.SemaphoreType.DMA((6,)),
+    ]
+    results = pl.pallas_call(
+        functools.partial(reduce_kernel, count, ORDERS),
+        out_shape=[jax.ShapeDtypeStruct(s, jnp.float32) for s in sizes]
+        + [jax.ShapeDtypeStruct((8, 128), jnp.float32)],
+        in_specs=[any_spec] * count,
+        out_specs=[vmem] * (count + 1),
+        scratch_shapes=scratch,
+        compiler_params=pltpu.CompilerParams(
+            collective_id=1, has_side_effects=True, vmem_limit_bytes=48 * 1024 * 1024
+        ),
+        name="reduce",
+    )(*split)
+    return results[:count], results[count][0, 0]
+
+
 def pack_shard(heads, merge, expand, shrink):
-    parts = [heads[0], heads[1], heads[2], merge.T, expand, shrink.T]
-    return jnp.concatenate([part.astype(jnp.bfloat16) for part in parts], axis=1)
-
-
-def unpack_shard(rows):
-    width = rows.shape[1] // 12
-    heads = jnp.stack([rows[:, 0:width], rows[:, width : 2 * width], rows[:, 2 * width : 3 * width]])
-    merge = rows[:, 3 * width : 4 * width].T
-    expand = rows[:, 4 * width : 8 * width]
-    shrink = rows[:, 8 * width : 12 * width].T
-    return (heads, merge, expand, shrink)
-
-
-def gather_block(rows):
-    gathered = lax.all_gather(rows, ("dp", "tensor"), axis=0, tiled=False)
-    split = gathered.reshape(lax.axis_size("dp"), 2, rows.shape[0], rows.shape[1])
-    return split.transpose(1, 0, 2, 3).reshape(2, -1, rows.shape[1])
+    first = jnp.concatenate([heads[0], heads[1], heads[2], merge.T], axis=1)
+    return [part.astype(jnp.bfloat16) for part in (first, expand, shrink.T)]
+
+
+def unpack_shard(parts):
+    first, expand, shrink = parts
+    width = first.shape[1] // 4
+    heads = jnp.stack([first[:, part * width : (part + 1) * width] for part in range(3)])
+    return (heads, first[:, 3 * width :].T, expand, shrink.T)
 
 
 def weight_views(packed):
-    width = packed.shape[2] // 12
-
-    def join(first, last):
-        return jnp.concatenate([packed[0, :, first:last], packed[1, :, first:last]], axis=1)
-
-    heads = jnp.stack([join(part * width, (part + 1) * width) for part in range(3)])
-    merge = join(3 * width, 4 * width)
-    expand = join(4 * width, 8 * width)
-    shrink = join(8 * width, 12 * width)
-    return (heads, merge, expand, shrink)
+    first, expand, shrink = packed
+    width = first.shape[2] // 4
+
+    def join(array):
+        return jnp.concatenate([array[0], array[1]], axis=1)
+
+    heads = jnp.stack([join(first[:, :, part * width : (part + 1) * width]) for part in range(3)])
+    return (heads, join(first[:, :, 3 * width :]), join(expand), join(shrink))
 
 
 def pack_grads(heads, merge, expand, shrink):
@@ -239,15 +522,8 @@
         half = array.shape[1] // 2
         return jnp.stack([array[:, :half], array[:, half:]])
 
-    parts = [halves(part) for part in (heads[0], heads[1], heads[2], merge, expand, shrink)]
-    return jnp.concatenate(parts, axis=2).astype(jnp.bfloat16)
-
-
-def reduce_block(packed):
-    dp_size = lax.axis_size("dp")
-    split = packed.reshape(2, dp_size, -1, packed.shape[2]).transpose(1, 0, 2, 3)
-    split = split.reshape(-1, packed.shape[2])
-    return lax.psum_scatter(split, ("dp", "tensor"), scatter_dimension=0, tiled=True).astype(jnp.float32)
+    first = jnp.concatenate([halves(part) for part in (heads[0], heads[1], heads[2], merge)], axis=2)
+    return [part.astype(jnp.bfloat16) for part in (first, halves(expand), halves(shrink))]
 
 
 def swap_half(rows):
@@ -258,9 +534,33 @@
     return lax.dynamic_index_in_dim(pair, index, axis=0, keepdims=False)
 
 
-def join_frame(pair):
+def is_tuned():
+    return lax.axis_size("dp") == 16 and lax.axis_size("tensor") == 2
+
+
+def gather_plain(shards, frames, cotangent, codes):
+    full = []
+    for shard in shards:
+        gathered = lax.all_gather(shard, ("dp", "tensor"), axis=0, tiled=False)
+        split = gathered.reshape((lax.axis_size("dp"), 2) + shard.shape)
+        full.append(split.transpose(1, 0, 2, 3).reshape(2, -1, shard.shape[1]))
     mine = lax.axis_index("tensor")
-    return jnp.concatenate([pick_frame(pair, mine), swap_half(pick_frame(pair, 1 - mine))], axis=0)
+    swapped = [swap_half(pick_frame(pair, 1 - mine)) for pair in (frames, cotangent, codes)]
+    return full, swapped[0], swapped[1], swapped[2]
+
+
+def reduce_plain(partials):
+    dp_size = lax.axis_size("dp")
+    sums = []
+    squares = jnp.zeros((), jnp.float32)
+    for partial in partials:
+        split = partial.reshape(2, dp_size, -1, partial.shape[2]).transpose(1, 0, 2, 3)
+        split = split.reshape(-1, partial.shape[2])
+        total = lax.psum_scatter(split, ("dp", "tensor"), scatter_dimension=0, tiled=True)
+        total = total.astype(jnp.float32)
+        squares = squares + jnp.sum(total * total)
+        sums.append(total)
+    return sums, lax.psum(squares, ("dp", "tensor"))
 
 
 def split_frame(rows):
@@ -269,6 +569,13 @@
     other = swap_half(rows[half:].astype(jnp.bfloat16)).astype(jnp.float32)
     own = rows[:half]
     return jnp.where(mine == 0, jnp.stack([own, other]), jnp.stack([other, own]))
+
+
+def small_rows(flat, row_count):
+    width = -(-flat.shape[-1] // (row_count * 128)) * 128
+    short = row_count * width - flat.shape[-1]
+    lead = [(0, 0)] * (flat.ndim - 1)
+    return jnp.pad(flat, lead + [(0, short)]).reshape(flat.shape[:-1] + (row_count, width))
 
 
 def adam_update(master, gradient, first_state, second_state, step_rate, decay_rate):
@@ -313,13 +620,28 @@
     codebook_second,
     decode_second,
 ):
-    own_rows = [
-        pack_shard(heads_weight[b], merge_weight[b], expand_weight[b], shrink_weight[b])
-        for b in range(2)
-    ]
+    shards = []
+    for b in range(2):
+        shards += pack_shard(heads_weight[b], merge_weight[b], expand_weight[b], shrink_weight[b])
+    row_count = shards[0].shape[0]
     small_parts = [vectors, encode_weight, codebook, decode_weight]
     small_flat = jnp.concatenate([part.astype(jnp.bfloat16).reshape(-1) for part in small_parts])
-    small_all = lax.all_gather(small_flat, ("dp", "tensor"), axis=0, tiled=False)
+    small_size = small_flat.shape[0]
+    shards.append(small_rows(small_flat, row_count))
+    code_tiles = codes.reshape(codes.shape[0], -1, 128)
+    mine = lax.axis_index("tensor")
+    gather = gather_tuned if is_tuned() else gather_plain
+    full, frame_other, cotangent_other, codes_other = gather(
+        shards, frames, out_cotangent, code_tiles
+    )
+    frame_rows = jnp.concatenate([pick_frame(frames, mine), frame_other], axis=0)
+    frame_rows = frame_rows.astype(jnp.float32)
+    cotangent = jnp.concatenate([pick_frame(out_cotangent, mine), cotangent_other], axis=0)
+    cotangent = cotangent.astype(jnp.float32)
+    code_ids = jnp.concatenate([pick_frame(code_tiles, mine), codes_other], axis=0).reshape(-1)
+    device_count = lax.axis_size("dp") * lax.axis_size("tensor")
+    small_all = full[6].reshape(2, -1, row_count * full[6].shape[2]).transpose(1, 0, 2)
+    small_all = small_all.reshape(device_count, -1)
     small_low = []
     offset = 0
     for part, cut_dim in zip(small_parts, (1, 0, 0, 1)):
@@ -332,10 +654,7 @@
         small_low.append(piece)
     vector_set = small_low[0].astype(jnp.float32)
     small_set = (vector_set, small_low[1], small_low[2], small_low[3])
-    frame_rows = join_frame(frames).astype(jnp.float32)
-    code_ids = join_frame(codes)
-    cotangent = join_frame(out_cotangent).astype(jnp.float32)
-    weight_sets = [weight_views(gather_block(rows)) for rows in own_rows]
+    weight_sets = [weight_views(full[0:3]), weight_views(full[3:6])]
     block_rows = frame_rows.shape[0] // 2
     frame_id = lax.axis_index("dp") * frames.shape[0] + lax.axis_index("tensor")
     clip_ends = jnp.cumsum(clip_frames)
@@ -359,32 +678,29 @@
     )
     decoded_all = split_frame(decoded)
     frame_grads = split_frame(dframe)
-    reduced = [
-        unpack_shard(reduce_block(pack_grads(*grads))) for grads in (encoder_grads, decoder_grads)
-    ]
-    block_grads = [jnp.stack([first, second]) for first, second in zip(*reduced)]
-    device_count = lax.axis_size("dp") * lax.axis_size("tensor")
     dvectors = jnp.concatenate([encoder_vectors, decoder_vectors, quant_grads[0]], axis=0)
     small_new = (dvectors, quant_grads[1], quant_grads[2], quant_grads[3])
     columns = []
     for gradient, part, cut_dim in zip(small_new, small_parts, (1, 0, 0, 1)):
         if cut_dim == 1:
             gradient = gradient.reshape(part.shape[0], device_count, -1).transpose(1, 0, 2)
-        columns.append(gradient.reshape(device_count, -1))
-    small_sum = lax.psum_scatter(
-        jnp.concatenate(columns, axis=1), ("dp", "tensor"), scatter_dimension=0, tiled=True
-    )
-    small_sum = small_sum.reshape(-1)
+        columns.append(gradient.reshape(device_count, -1).astype(jnp.bfloat16))
+    small_grad = small_rows(jnp.concatenate(columns, axis=1), row_count)
+    small_grad = small_grad.reshape((-1, 2) + small_grad.shape[1:]).transpose(1, 0, 2, 3)
+    small_grad = small_grad.reshape(2, -1, small_grad.shape[3])
+    partials = pack_grads(*encoder_grads) + pack_grads(*decoder_grads) + [small_grad]
+    reduce = reduce_tuned if is_tuned() else reduce_plain
+    sums, squares = reduce(partials)
+    reduced = [unpack_shard(sums[0:3]), unpack_shard(sums[3:6])]
+    block_grads = [jnp.stack([first, second]) for first, second in zip(*reduced)]
+    small_sum = sums[6].reshape(-1)[:small_size]
     small_grads = []
     offset = 0
     for part in small_parts:
         small_grads.append(small_sum[offset : offset + part.size].reshape(part.shape))
         offset += part.size
     gradients = tuple(block_grads) + tuple(small_grads)
-    local_squares = jnp.zeros((), jnp.float32)
-    for gradient in gradients:
-        local_squares = local_squares + jnp.sum(gradient * gradient)
-    norm_before = jnp.sqrt(lax.psum(local_squares, ("dp", "tensor")))
+    norm_before = jnp.sqrt(squares)
     factor = MAX_NORM / jnp.maximum(norm_before, MAX_NORM)
     masters = (
         heads_weight,

time: 1100 us -> 693 us (0.63)
  waiting for transfers between devices: 481 us -> 0.01 us
  Pallas kernels: 0 us -> 182 us
  local copies, waits for them, and re-layouts: 148 us -> 106 us
  blocking collectives: 40.1 us -> 0 us
  between operations: 25.7 us -> 6.91 us
    reduce_scatter x2 -> x0, waiting for transfers between devices: 235 us -> none  [reduce_block(): lax.psum_scatter(split, ('dp', 'tensor'), scatter_dimension=0, tiled=True)]
    pallas_call x0 -> x2, Pallas kernels: none -> 182 us  [the longest x1 92.1 us: gather_tuned(): pl.pallas_call(functools.partial(gather_kernel, count, ORDERS), out_shape...]
    unnamed x8 -> x0, waiting for transfers between devices: 181 us -> none
    all_gather x2 -> x0, waiting for transfers between devices: 51.1 us -> none  [gather_block(): gathered = lax.all_gather(rows, ('dp', 'tensor'), axis=0, tiled=False)]
    psum x1 -> x0, blocking collectives: 40.1 us -> none  [local(): norm_before = jnp.sqrt(lax.psum(local_squares, ('dp', 'tensor')))]
    dot_general x5 -> x0, local copies, waits for them, and re-layouts: 14.6 us -> none  [the longest x4 11.3 us: fast_dot(): jnp.einsum(formula, first_arg, second_arg, preferred_element_type=jnp.flo...]
    ppermute x5 -> x2, waiting for transfers between devices: 13.8 us -> 0.01 us  [swap_half(): return lax.ppermute(rows, 'tensor', [(0, 1), (1, 0)])]
    transpose x6 -> x2, local copies, waits for them, and re-layouts: 13 us -> 0.09 us  [the longest x1 0.09 us: local(): small_grad.reshape((-1, 2) + small_grad.shape[1:]).transpose(1, 0, 2, 3)]
  transfers between devices with their start and end apart: 11 -> 2, of which waited for: 7 -> 0; matrix products, arithmetic and copies ran while one was open for 19% -> 13% of each run, Pallas kernels for 0% -> 13%
where the time goes in v2:
time: 693 us; the launch traced here: 682 us
  matrix products  259 us (37%)
  Pallas kernels  182 us (26%)
  other arithmetic  127 us (18%)
  local copies, waits for them, and re-layouts  106 us (15%)
    dot_general x50, matrix products, fast_dot(): jnp.einsum(formula, first_arg, second_arg, preferred_element_type=jnp.flo...  248 us
    pallas_call x1, Pallas kernels, gather_tuned(): pl.pallas_call(functools.partial(gather_kernel, count, ORDERS), out_shape...  92.1 us
    pallas_call x1, Pallas kernels, reduce_tuned(): pl.pallas_call(functools.partial(reduce_kernel, count, ORDERS), out_shape...  89.4 us
    unnamed x542, local copies, waits for them, and re-layouts  49.6 us
    convert_element_type x4, other arithmetic, attend_backward(): dscores = (attend * (dattend - inner_sum)).astype(jnp.bfloat16)  43.7 us
    another operation x6, local copies, waits for them, and re-layouts, attend_backward(): jnp.stack([jnp.concatenate(dqueries, 0).reshape(length, width), dkeys_all...  14.1 us
  transfers between devices with their start and end apart: 2, of which 0 were waited for; matrix products, arithmetic and copies ran while one was open for 13% of the time, Pallas kernels for 13%

profile of v2, /device:TPU:0, one launch (start us, length us, event | category | flops | bytes accessed | tf_op | source)
XLA Modules:
  0.0 682.4 jit_solution(15574642671485061667)
XLA Ops:
  9.3 92.1 %gather.8 = (bf16[2,4,2,2,32,1024]{5,4,3,2,1,0:T(8,128)(2,1)}, bf16[2,4,2,2,32,1024]{5,4,3,2,1,0:T(8,128)(2,1)}, bf16[2,4,2,2,32,1024]{5,4,3,2,1,0:T(8,128)(2,1)...) custom-call(bf16[32,1024]{1,0:T(8,128)(2,1)} %get-tuple-element.309., ...), custom_call_target="tpu_custom_call" | custom-call | tf_op jit(solution)/shard_map/gather/pallas_call | solution.py:318
  108.6 3.2 gather_fusion
  130.4 3.4 fusion
  136.2 5.2 fusion.72
  143.9 3.4 fusion.1
  149.6 5.0 fusion.71
  166.8 3.3 copy-done.233
  170.1 8.9 %fusion.22 = bf16[1024,2048]{1,0:T(8,128)(2,1)} fusion(f32[1024,2048]{1,0:T(8,128)S(1)} %fusion.64, bf16[512,1024]{1,0:T(8,128)(2,1)S(1)} %bitcast.424, bf16[512,1024]{1,0:T(8,128)(2,1)S(1)} %bitcast.422, bf16[512,512]{1,0:T(8,128)(2,1)S(1)} %copy-done.45, bf16[512,512]{1,0:T(8,128)(2,1)S(1)} %get-tuple-element.217), kind=kOutput, calls=%fused_computation.48 | convolution fusion | flops 2195718144 | bytes 15728640 | tf_op jit(solution)/shard_map/td,df->tf/dot_general | solution.py:42
  179.0 5.8 multiply_reduce_fusion.10
  188.1 9.2 %multiply_reduce_fusion.1 = (f32[8,512]{1,0:T(8,128)S(1)}, f32[8,512,1024]{2,1,0:T(8,128)}) fusion(f32[8,512,1024]{2,1,0:T(8,128)S(1)} %bitcast.338, f32[8,512]{1,0:T(8,128)S(1)} %log_add_fusion.1, bf16[512,8,64]{0,2,1:T(8,128)(2,1)} %bitcast.367, bf16[1024,8,64]{0,2,1:T(8,128)(2,1)S(1)} %bitcast.355), kind=kOutput, calls=%fused_computation.6 | convolution fusion | flops 553644032 | bytes 35160064 | tf_op jit(solution)/shard_map/qhd,khd->hqk/dot_general | solution.py:42
  197.2 10.6 %multiply_convert_fusion.1 = bf16[8,512,1024]{2,1,0:T(8,128)(2,1)} fusion(f32[8,512,1024]{2,1,0:T(8,128)} %get-tuple-element.295, f32[8,512,1024]{2,1,0:T(8,128)S(1)} %bitcast.338, f32[8,512]{1,0:T(8,128)S(1)} %get-tuple-element.294, f32[8,512]{1,0:T(8,128)S(1)} %log_add_fusion.1), kind=kLoop, calls=%fused_computation.5 | loop fusion | flops 20971520 | bytes 41975808 | tf_op jit(solution)/shard_map/convert_element_type | solution.py:95
  207.8 7.0 %fusion.76 = bf16[512,8,64]{0,2,1:T(8,128)(2,1)} fusion(bf16[1024,8,64]{0,2,1:T(8,128)(2,1)S(1)} %bitcast.347, bf16[8,512,1024]{2,1,0:T(8,128)(2,1)} %multiply_convert_fusion.1), kind=kOutput, calls=%fused_computation.175 | convolution fusion | flops 537395200 | bytes 9961472 | tf_op jit(solution)/shard_map/hqk,khd->qhd/dot_general | solution.py:42
  217.8 13.8 %multiply_reduce_fusion = (f32[8,512]{1,0:T(8,128)}, f32[8,512,1024]{2,1,0:T(8,128)}) fusion(f32[8,512,1024]{2,1,0:T(8,128)} %copy-done.3, f32[8,512]{1,0:T(8,128)S(1)} %log_add_fusion, bf16[512,8,64]{0,2,1:T(8,128)(2,1)} %bitcast.371, bf16[1024,8,64]{0,2,1:T(8,128)(2,1)S(1)} %bitcast.356), kind=kOutput, calls=%fused_computation.3 | convolution fusion | flops 553644032 | bytes 35160064 | tf_op jit(solution)/shard_map/qhd,khd->hqk/dot_general | solution.py:42
  231.6 5.5 fusion.8
  253.6 3.5 multiply_reduce_fusion.5
  257.1 3.4 fusion.2
  263.0 5.0 fusion.70
  270.5 3.4 fusion.3
  276.3 5.4 fusion.69
  282.3 11.9 %multiply_convert_fusion = bf16[8,512,1024]{2,1,0:T(8,128)(2,1)S(1)} fusion(f32[8,512,1024]{2,1,0:T(8,128)} %get-tuple-element.297, f32[8,512,1024]{2,1,0:T(8,128)} %copy-done.3, f32[8,512]{1,0:T(8,128)S(1)} %copy-done.127, f32[8,512]{1,0:T(8,128)S(1)} %copy-done.111), kind=kLoop, calls=%fused_computation.2 | loop fusion | flops 20971520 | bytes 41975808 | tf_op jit(solution)/shard_map/convert_element_type | solution.py:95
  300.9 6.1 multiply_convert_fusion.6
  309.5 10.0 %add_convert_fusion = bf16[8,64,1024]{2,1,0:T(8,128)(2,1)} fusion(f32[8,64,1024]{2,1,0:T(8,128)S(1)} %copy-done.29, bf16[512,8,64]{0,2,1:T(8,128)(2,1)} %bitcast.368, f32[8,512,1024]{2,1,0:T(8,128)} %copy-done.2, f32[8,512]{1,0:T(8,128)S(1)} %copy-done.109), kind=kOutput, calls=%fused_computation.123 | convolution fusion | flops 550502400 | bytes 20463616 | tf_op jit(solution)/shard_map/hqk,qhd->khd/dot_general | solution.py:42
  322.0 5.1 multiply_reduce_fusion.8
  341.9 6.2 fusion.199
  354.4 4.9 fusion.167
  359.4 4.0 fusion.100
  367.6 10.5 %fusion.29 = bf16[1024,2048]{1,0:T(8,128)(2,1)S(1)} fusion(f32[1024,2048]{1,0:T(8,128)} %copy-done.234, bf16[512,1024]{1,0:T(8,128)(2,1)S(1)} %bitcast.433, bf16[512,1024]{1,0:T(8,128)(2,1)S(1)} %bitcast.431, f32[1024,512]{1,0:T(8,128)S(1)} %get-tuple-element.163, f32[1024]{0:T(1024)S(1)} %negate_multiply_fusion.4), kind=kOutput, calls=%fused_computation.55 | convolution fusion | flops 2194669568 | bytes 16781312 | tf_op jit(solution)/shard_map/td,df->tf/dot_general | solution.py:42
  378.2 3.4 multiply_reduce_fusion.11
  386.2 10.3 %multiply_reduce_fusion.3 = (f32[8,512]{1,0:T(8,128)}, f32[8,512,1024]{2,1,0:T(8,128)}) fusion(f32[8,512,1024]{2,1,0:T(8,128)S(1)} %bitcast.334, f32[8,512]{1,0:T(8,128)S(1)} %log_add_fusion.3, bf16[512,8,64]{0,2,1:T(8,128)(2,1)} %bitcast.369, bf16[1024,8,64]{0,2,1:T(8,128)(2,1)} %bitcast.349), kind=kOutput, calls=%fused_computation.12 | convolution fusion | flops 553644032 | bytes 35160064 | tf_op jit(solution)/shard_map/qhd,khd->hqk/dot_general | solution.py:42
  396.5 10.7 %multiply_convert_fusion.3 = bf16[8,512,1024]{2,1,0:T(8,128)(2,1)} fusion(f32[8,512,1024]{2,1,0:T(8,128)} %get-tuple-element.305, f32[8,512,1024]{2,1,0:T(8,128)S(1)} %bitcast.334, f32[8,512]{1,0:T(8,128)} %get-tuple-element.304, f32[8,512]{1,0:T(8,128)S(1)} %log_add_fusion.3), kind=kLoop, calls=%fused_computation.11 | loop fusion | flops 20971520 | bytes 41975808 | tf_op jit(solution)/shard_map/convert_element_type | solution.py:95
  407.2 7.0 %fusion.78 = bf16[512,8,64]{0,2,1:T(8,128)(2,1)} fusion(bf16[1024,8,64]{0,2,1:T(8,128)(2,1)S(1)} %bitcast.343, bf16[8,512,1024]{2,1,0:T(8,128)(2,1)} %multiply_convert_fusion.3), kind=kOutput, calls=%fused_computation.177 | convolution fusion | flops 537395200 | bytes 9961472 | tf_op jit(solution)/shard_map/hqk,khd->qhd/dot_general | solution.py:42
  417.1 14.2 %multiply_reduce_fusion.2 = (f32[8,512]{1,0:T(8,128)}, f32[8,512,1024]{2,1,0:T(8,128)}) fusion(f32[8,512,1024]{2,1,0:T(8,128)} %copy-done.1, f32[8,512]{1,0:T(8,128)} %log_add_fusion.2, bf16[512,8,64]{0,2,1:T(8,128)(2,1)} %bitcast.373, bf16[1024,8,64]{0,2,1:T(8,128)(2,1)} %bitcast.350), kind=kOutput, calls=%fused_computation.9 | convolution fusion | flops 553644032 | bytes 35160064 | tf_op jit(solution)/shard_map/qhd,khd->hqk/dot_general | solution.py:42
  431.3 5.2 fusion.12
  436.5 10.6 %multiply_convert_fusion.2 = bf16[8,512,1024]{2,1,0:T(8,128)(2,1)} fusion(f32[8,512,1024]{2,1,0:T(8,128)} %get-tuple-element.307, f32[8,512,1024]{2,1,0:T(8,128)S(1)} %bitcast.336, f32[8,512]{1,0:T(8,128)S(1)} %copy-done.128, f32[8,512]{1,0:T(8,128)S(1)} %copy-done.107), kind=kLoop, calls=%fused_computation.8 | loop fusion | flops 20971520 | bytes 41975808 | tf_op jit(solution)/shard_map/convert_element_type | solution.py:95
  447.1 6.1 fusion.77
  456.7 6.5 multiply_convert_fusion.7
  465.6 9.2 %add_convert_fusion.1 = bf16[8,64,1024]{2,1,0:T(8,128)(2,1)} fusion(f32[8,64,1024]{2,1,0:T(8,128)} %fusion.12, bf16[512,8,64]{0,2,1:T(8,128)(2,1)S(1)} %bitcast.370, f32[8,512,1024]{2,1,0:T(8,128)} %copy-done, f32[8,512]{1,0:T(8,128)S(1)} %log_add_fusion.3), kind=kOutput, calls=%fused_computation.128 | convolution fusion | flops 550502400 | bytes 20463616 | tf_op jit(solution)/shard_map/hqk,qhd->khd/dot_general | solution.py:42
  477.1 4.9 bitcast_reduce_fusion.1
  489.9 7.6 %add_add_fusion.10 = f32[1024,512]{1,0:T(8,128)S(1)} fusion(f32[1024,512]{1,0:T(8,128)} %copy-done.21, bf16[512,1024]{1,0:T(8,128)(2,1)} %bitcast.425, bf16[512,1024]{1,0:T(8,128)(2,1)} %bitcast.423, f32[512]{0:T(512)S(1)} %add.458, f32[1024,2048]{1,0:T(8,128)} %copy-done.233), kind=kOutput, calls=%fused_computation.138 | convolution fusion | flops 2171600896 | bytes 14682112 | tf_op jit(solution)/shard_map/tf,df->td/dot_general | solution.py:42
  504.2 3.2 convolution_convert_fusion.8
  507.6 6.4 convolution_convert_fusion.1
  514.1 3.2 convolution_bitcast_fusion
  519.3 5.0 convolution_convert_fusion.2
  524.4 4.0 convolution_convert_fusion.3
  528.5 3.3 convolution_bitcast_fusion.1
  532.6 4.6 convolution_convert_fusion
  537.5 8.4 %scatter_custom_fusion = f32[8192,32]{1,0:T(8,128)} fusion(s32[1024]{0:T(1024)} %get-tuple-element.275, f32[1024,32]{1,0:T(8,128)S(1)} %copy.213, f32[]{:T(128)} %constant.63.clone.1), kind=kCustom, calls=%fused_computation.116 | custom fusion | flops 32768 | bytes 1049088 | tf_op jit(solution)/shard_map/scatter-add | solution.py:196
  570.4 89.4 %reduce.7 = (f32[32,1024]{1,0:T(8,128)S(1)}, f32[32,1024]{1,0:T(8,128)S(1)}, f32[32,1024]{1,0:T(8,128)S(1)}, f32[32,1024]{1,0:T(8,128)S(1)}, f32[32,1024]{1,0:T(...) custom-call(bf16[2,4,2,2,32,1024]{5,4,3,2,1,0:T(8,128)(2,1)S(1)} %maximum_maximum_fusion.refs_0_, ...), custom_call_target="tpu_custom_call" | custom-call | tf_op jit(solution)/shard_map/reduce/pallas_call | solution.py:482
  (797 shorter events, 196.4 us)
Async XLA Ops:
  103.4 9.9 %copy-start.129 = (pred[1024]{0:T(1024)(128)(4,1)}, pred[1024]{0:T(1024)(128)(4,1)S(1)}, u32[]{:S(2)}) copy-start(pred[1024]{0:T(1024)(128)(4,1)S(1)} %compare_and_fusion) | copy-start | bytes 3076
  112.9 41.8 %copy-start.159 = (f32[512]{0:T(512)}, f32[512]{0:T(512)S(1)}, u32[]{:S(2)}) copy-start(f32[512]{0:T(512)S(1)} %add.440) | copy-start | bytes 6148
  113.9 9.8 %copy-start.10 = (f32[1024,512]{1,0:T(8,128)}, f32[1024,512]{1,0:T(8,128)S(1)}, u32[]{:S(2)}) copy-start(f32[1024,512]{1,0:T(8,128)S(1)} %get-tuple-element.278) | copy-start | bytes 6291460
  113.9 9.7 %copy-start.151 = (f32[1024]{0:T(1024)}, f32[1024]{0:T(1024)S(1)}, u32[]{:S(2)}) copy-start(f32[1024]{0:T(1024)S(1)} %broadcast_multiply_fusion.4) | copy-start | bytes 12292
  127.2 14.2 %copy-start.34 = (bf16[1,512,512]{1,2,0:T(8,128)(2,1)}, bf16[1,512,512]{1,2,0:T(8,128)(2,1)S(1)}, u32[]{:S(2)}) copy-start(bf16[1,512,512]{1,2,0:T(8,128)(2,1)S(1)} %get-tuple-element.174) | copy-start | bytes 1572868
  127.9 38.8 %copy-start.48 = (bf16[512,512]{1,0:T(8,128)(2,1)}, bf16[512,512]{1,0:T(8,128)(2,1)S(1)}, u32[]{:S(2)}) copy-start(bf16[512,512]{1,0:T(8,128)(2,1)S(1)} %get-tuple-element.217) | copy-start | bytes 1572868
  133.9 63.3 %copy-start.108 = (f32[8,512]{1,0:T(8,128)}, f32[8,512]{1,0:T(8,128)S(1)}, u32[]{:S(2)}) copy-start(f32[8,512]{1,0:T(8,128)S(1)} %log_add_fusion.1) | copy-start | bytes 49156
  154.6 76.9 %copy-start.110 = (f32[8,512]{1,0:T(8,128)}, f32[8,512]{1,0:T(8,128)S(1)}, u32[]{:S(2)}) copy-start(f32[8,512]{1,0:T(8,128)S(1)} %log_add_fusion) | copy-start | bytes 49156
  157.6 27.1 %copy-start.154 = (f32[1024]{0:T(1024)}, f32[1024]{0:T(1024)S(1)}, u32[]{:S(2)}) copy-start(f32[1024]{0:T(1024)S(1)} %broadcast_multiply_fusion.3) | copy-start | bytes 12292
  159.4 25.4 %copy-start.189 = (f32[1024]{0:T(1024)}, f32[1024]{0:T(1024)S(1)}, u32[]{:S(2)}) copy-start(f32[1024]{0:T(1024)S(1)} %fusion.111) | copy-start | bytes 12292
  159.5 25.2 %copy-start.199 = (f32[512]{0:T(512)}, f32[512]{0:T(512)S(1)}, u32[]{:S(2)}) copy-start(f32[512]{0:T(512)S(1)} %mul.852) | copy-start | bytes 6148
  214.8 16.7 %slice-start.12 = ((s8[16777216]{0:T(1024)(128)(4,1)}), s8[4194304]{0:T(1024)(128)(4,1)S(1)}, s32[]{:S(2)}) async-start(s8[16777216]{0:T(1024)(128)(4,1)} %bitcast.339), calls=%async_computation.12 | async-start | bytes 8388608
  214.8 16.7 %slice-start.13 = ((s8[16777216]{0:T(1024)(128)(4,1)}), s8[4194304]{0:T(1024)(128)(4,1)S(1)}, s32[]{:S(2)}) async-start(s8[16777216]{0:T(1024)(128)(4,1)} %bitcast.339), calls=%async_computation.13 | async-start | bytes 8388608
  217.8 13.8 %slice-start.14 = ((s8[16777216]{0:T(1024)(128)(4,1)}), s8[4194304]{0:T(1024)(128)(4,1)S(1)}, s32[]{:S(2)}) async-start(s8[16777216]{0:T(1024)(128)(4,1)} %bitcast.339), calls=%async_computation.14 | async-start | bytes 8388608
  217.8 13.8 %slice-start.15 = ((s8[16777216]{0:T(1024)(128)(4,1)}), s8[4194304]{0:T(1024)(128)(4,1)S(1)}, s32[]{:S(2)}) async-start(s8[16777216]{0:T(1024)(128)(4,1)} %bitcast.339), calls=%async_computation.15 | async-start | bytes 8388608
  237.4 10.9 %copy-start.131 = (f32[1024]{0:T(1024)}, f32[1024]{0:T(1024)S(1)}, u32[]{:S(2)}) copy-start(f32[1024]{0:T(1024)S(1)} %broadcast_multiply_fusion.2) | copy-start | bytes 12292
  237.9 10.3 %copy-start.139 = (f32[1024]{0:T(1024)}, f32[1024]{0:T(1024)S(1)}, u32[]{:S(2)}) copy-start(f32[1024]{0:T(1024)S(1)} %fusion.112) | copy-start | bytes 12292
  239.6 90.5 %copy-start.66 = (bf16[512,256]{1,0:T(8,128)(2,1)}, bf16[512,256]{1,0:T(8,128)(2,1)S(1)}, u32[]{:S(2)}) copy-start(bf16[512,256]{1,0:T(8,128)(2,1)S(1)} %get-tuple-element.188) | copy-start | bytes 786436
  252.4 15.5 %copy-start.7 = (bf16[1,1024,512]{1,2,0:T(8,128)(2,1)}, bf16[1,1024,512]{1,2,0:T(8,128)(2,1)S(1)}, u32[]{:S(2)}) copy-start(bf16[1,1024,512]{1,2,0:T(8,128)(2,1)S(1)} %get-tuple-element.171) | copy-start | bytes 3145732
  309.5 12.5 %copy-start.152 = (f32[1024]{0:T(1024)S(1)}, f32[1024]{0:T(1024)}, u32[]{:S(2)}) copy-start(f32[1024]{0:T(1024)} %copy-done.151) | copy-start | bytes 12292
  309.5 12.5 %copy-start.160 = (f32[512]{0:T(512)S(1)}, f32[512]{0:T(512)}, u32[]{:S(2)}) copy-start(f32[512]{0:T(512)} %copy-done.159) | copy-start | bytes 6148
  309.5 12.5 %copy-start.187 = (f32[1024]{0:T(1024)S(1)}, f32[1024]{0:T(1024)}, u32[]{:S(2)}) copy-start(f32[1024]{0:T(1024)} %copy-done.186) | copy-start | bytes 12292
  309.5 12.5 %copy-start.197 = (f32[512]{0:T(512)S(1)}, f32[512]{0:T(512)}, u32[]{:S(2)}) copy-start(f32[512]{0:T(512)} %copy-done.196) | copy-start | bytes 6148
  351.5 11.9 %copy-start.60 = (f32[1024,32]{0,1:T(8,128)}, f32[1024,32]{0,1:T(8,128)S(1)}, u32[]{:S(2)}) copy-start(f32[1024,32]{0,1:T(8,128)S(1)} %get-tuple-element.300) | copy-start | bytes 393220
  351.5 11.9 %copy-start.133 = (f32[1024]{0:T(1024)}, f32[1024]{0:T(1024)S(1)}, u32[]{:S(2)}) copy-start(f32[1024]{0:T(1024)S(1)} %add_rsqrt_fusion) | copy-start | bytes 12292
  367.3 15.3 %copy-start.19 = (f32[1024,512]{1,0:T(8,128)}, f32[1024,512]{1,0:T(8,128)S(1)}, u32[]{:S(2)}) copy-start(f32[1024,512]{1,0:T(8,128)S(1)} %get-tuple-element.163) | copy-start | bytes 6291460
  367.3 15.3 %copy-start.194 = (f32[1024]{0:T(1024)}, f32[1024]{0:T(1024)S(1)}, u32[]{:S(2)}) copy-start(f32[1024]{0:T(1024)S(1)} %negate_multiply_fusion.4) | copy-start | bytes 12292
  367.5 10.6 %copy-start.25 = (f32[1024,512]{1,0:T(8,128)S(1)}, f32[1024,512]{1,0:T(8,128)}, u32[]{:S(2)}) copy-start(f32[1024,512]{1,0:T(8,128)} %copy-done.24) | copy-start | bytes 6291460
  367.5 10.6 %copy-start.89 = (bf16[1,4,2,2,32,1024]{5,4,3,2,1,0:T(8,128)(2,1)S(1)}, bf16[1,4,2,2,32,1024]{5,4,3,2,1,0:T(8,128)(2,1)}, u32[]{:S(2)}) copy-start(bf16[1,4,2,2,32,1024]{5,4,3,2,1,0:T(8,128)(2,1)} %get-tuple-element.196) | copy-start | bytes 3145732
  367.5 10.6 %copy-start.91 = (bf16[1,4,2,2,32,1024]{5,4,3,2,1,0:T(8,128)(2,1)S(1)}, bf16[1,4,2,2,32,1024]{5,4,3,2,1,0:T(8,128)(2,1)}, u32[]{:S(2)}) copy-start(bf16[1,4,2,2,32,1024]{5,4,3,2,1,0:T(8,128)(2,1)} %get-tuple-element.197) | copy-start | bytes 3145732
  367.5 10.6 %copy-start.157 = (f32[1024]{0:T(1024)S(1)}, f32[1024]{0:T(1024)}, u32[]{:S(2)}) copy-start(f32[1024]{0:T(1024)} %copy-done.156) | copy-start | bytes 12292
  367.6 10.6 %copy-start.192 = (f32[1024]{0:T(1024)S(1)}, f32[1024]{0:T(1024)}, u32[]{:S(2)}) copy-start(f32[1024]{0:T(1024)} %copy-done.191) | copy-start | bytes 12292
  367.6 10.6 %copy-start.202 = (f32[512]{0:T(512)S(1)}, f32[512]{0:T(512)}, u32[]{:S(2)}) copy-start(f32[512]{0:T(512)} %copy-done.201) | copy-start | bytes 6148
  396.5 10.7 %copy-start.8 = (bf16[1,1024,512]{1,2,0:T(8,128)(2,1)S(1)}, bf16[1,1024,512]{1,2,0:T(8,128)(2,1)}, u32[]{:S(2)}) copy-start(bf16[1,1024,512]{1,2,0:T(8,128)(2,1)} %copy-done.7) | copy-start | bytes 3145732
  414.2 17.1 %slice-start.4 = ((s8[16777216]{0:T(1024)(128)(4,1)}), s8[4194304]{0:T(1024)(128)(4,1)S(1)}, s32[]{:S(2)}) async-start(s8[16777216]{0:T(1024)(128)(4,1)} %bitcast.335), calls=%async_computation.4 | async-start | bytes 8388608
  414.2 17.1 %slice-start.5 = ((s8[16777216]{0:T(1024)(128)(4,1)}), s8[4194304]{0:T(1024)(128)(4,1)S(1)}, s32[]{:S(2)}) async-start(s8[16777216]{0:T(1024)(128)(4,1)} %bitcast.335), calls=%async_computation.5 | async-start | bytes 8388608
  417.1 14.2 %slice-start.6 = ((s8[16777216]{0:T(1024)(128)(4,1)}), s8[4194304]{0:T(1024)(128)(4,1)S(1)}, s32[]{:S(2)}) async-start(s8[16777216]{0:T(1024)(128)(4,1)} %bitcast.335), calls=%async_computation.6 | async-start | bytes 8388608
  417.1 14.2 %slice-start.7 = ((s8[16777216]{0:T(1024)(128)(4,1)}), s8[4194304]{0:T(1024)(128)(4,1)S(1)}, s32[]{:S(2)}) async-start(s8[16777216]{0:T(1024)(128)(4,1)} %bitcast.335), calls=%async_computation.7 | async-start | bytes 8388608
  436.5 10.6 %copy-start.9 = (bf16[1,1024,512]{1,2,0:T(8,128)(2,1)S(1)}, bf16[1,1024,512]{1,2,0:T(8,128)(2,1)}, u32[]{:S(2)}) copy-start(bf16[1,1024,512]{1,2,0:T(8,128)(2,1)} %copy-done.7) | copy-start | bytes 3145732
  489.1 186.4 %collective-permute-start.1 = (bf16[512,512]{1,0:T(8,128)(2,1)}, bf16[512,512]{1,0:T(8,128)(2,1)}, u32[]{:S(2)}, u32[]{:S(2)}) collective-permute-start(bf16[512,512]{1,0:T(8,128)(2,1)} %slice.787), channel_id=1, source_target_pairs={{0,1},{1,0},{2,3},{3,2},{4,5},{5,4},{6,7},{7,6},{8,9},{9,8},{10,11... | collective-permute-start | bytes 1572872 | tf_op jit(solution)/shard_map/ppermute | solution.py:530
  489.8 11.5 %copy-start.16 = (bf16[1024,512]{1,0:T(8,128)(2,1)S(1)}, bf16[1024,512]{1,0:T(8,128)(2,1)}, u32[]{:S(2)}) copy-start(bf16[1024,512]{1,0:T(8,128)(2,1)} %copy-done.15) | copy-start | bytes 3145732
  489.8 11.5 %copy-start.42 = (bf16[1024,32]{0,1:T(8,128)(2,1)S(1)}, bf16[1024,32]{0,1:T(8,128)(2,1)}, u32[]{:S(2)}) copy-start(bf16[1024,32]{0,1:T(8,128)(2,1)} %copy-done.40) | copy-start | bytes 196612
  489.8 11.5 %copy-start.61 = (f32[1024,32]{0,1:T(8,128)S(1)}, f32[1024,32]{0,1:T(8,128)}, u32[]{:S(2)}) copy-start(f32[1024,32]{0,1:T(8,128)} %copy-done.60) | copy-start | bytes 393220
  489.8 11.4 %copy-start.134 = (f32[1024]{0:T(1024)S(1)}, f32[1024]{0:T(1024)}, u32[]{:S(2)}) copy-start(f32[1024]{0:T(1024)} %copy-done.133) | copy-start | bytes 12292
  489.8 11.4 %copy-start.138 = (f32[1024]{0:T(1024)S(1)}, f32[1024]{0:T(1024)}, u32[]{:S(2)}) copy-start(f32[1024]{0:T(1024)} %copy-done.137) | copy-start | bytes 12292
  499.7 178.6 %collective-permute-start = (bf16[512,512]{1,0:T(8,128)(2,1)}, bf16[512,512]{1,0:T(8,128)(2,1)}, u32[]{:S(2)}, u32[]{:S(2)}) collective-permute-start(bf16[512,512]{1,0:T(8,128)(2,1)} %slice.788), channel_id=1, source_target_pairs={{0,1},{1,0},{2,3},{3,2},{4,5},{5,4},{6,7},{7,6},{8,9},{9,8},{10,11... | collective-permute-start | bytes 1572872 | tf_op jit(solution)/shard_map/ppermute | solution.py:530
  507.6 11.7 %slice-start.18 = ((s8[8388608]{0:T(1024)(128)(4,1)}), s8[4194304]{0:T(1024)(128)(4,1)S(1)}, s32[]{:S(2)}) async-start(s8[8388608]{0:T(1024)(128)(4,1)} %bitcast.457), calls=%async_computation.18 | async-start | bytes 8388608
  570.4 90.4 %copy-start.31 = (f32[1024,512]{1,0:T(8,128)S(1)}, f32[1024,512]{1,0:T(8,128)}, u32[]{:S(2)}) copy-start(f32[1024,512]{1,0:T(8,128)} %copy-done.30) | copy-start | bytes 6291460
  (211 other events, 860.5 us)
